TPU v7x, 32 devices: a whole 2x2x4 slice. The times are simulated.
32 devices in a mesh: img: 16 (over z, y, core), lat: 2 (over x).
Axes of the slice: x: 2, y: 2, z: 4, core: 2. Of those that a mesh axis runs over, the one named last changes fastest.
Arguments:
- patches: bfloat16 [128, 256, 1024], P('img', 'lat'), may hold values from -6 to 6
- latents: bfloat16 [128, 64, 1024], P('img', 'lat'), may hold values from -6 to 6
- cotangent: bfloat16 [128, 64, 1024], P('img', 'lat'), may hold values from -6 to 6
- doc_images: int32 [64], replicated, may hold values from 0 to 8, as said below
- doc_device: int32 [64], replicated, may hold values from 0 to 15, as said below
- query_weight: bfloat16 [1024, 512], replicated, may hold values from -0.1875 to 0.1875
- key_weight: bfloat16 [1024, 512], replicated, may hold values from -0.1875 to 0.1875
- value_weight: bfloat16 [1024, 512], replicated, may hold values from -0.1875 to 0.1875
- output_weight: bfloat16 [512, 1024], replicated, may hold values from -1 to 1
- up_weight: bfloat16 [1024, 4096], replicated, may hold values from -0.1875 to 0.1875
- down_weight: bfloat16 [4096, 1024], replicated, may hold values from -0.09375 to 0.09375
- media_gain: float32 [1024], replicated, may hold values from 0.25 to 1.75
- media_bias: float32 [1024], replicated, may hold values from -2 to 2
- latent_gain: float32 [1024], replicated, may hold values from 0.25 to 1.75
- latent_bias: float32 [1024], replicated, may hold values from -2 to 2
- ffn_gain: float32 [1024], replicated, may hold values from 0.25 to 1.75
- ffn_bias: float32 [1024], replicated, may hold values from -2 to 2
Outputs:
- new_latents: bfloat16 [128, 64, 1024], P('img', 'lat')
- patches_grad: float32 [128, 256, 1024], P('img', 'lat')
- latents_grad: float32 [128, 64, 1024], P('img', 'lat')
- query_grad: float32 [1024, 512], P(('img', 'lat'))
- key_grad: float32 [1024, 512], P(('img', 'lat'))
- value_grad: float32 [1024, 512], P(('img', 'lat'))
- output_grad: float32 [512, 1024], P(('img', 'lat'))
- up_grad: float32 [1024, 4096], P(('img', 'lat'))
- down_grad: float32 [4096, 1024], P(('img', 'lat'))
- media_gain_grad: float32 [1024], P(('img', 'lat'))
- media_bias_grad: float32 [1024], P(('img', 'lat'))
- latent_gain_grad: float32 [1024], P(('img', 'lat'))
- latent_bias_grad: float32 [1024], P(('img', 'lat'))
- ffn_gain_grad: float32 [1024], P(('img', 'lat'))
- ffn_bias_grad: float32 [1024], P(('img', 'lat'))
Inputs may be any that keep to these rules, and one draw needn't show every extreme that they name: `doc_images`: the documents that doc_device assigns to one index of img hold 8 images at most in all; on some index they hold exactly 8, all in one document. `doc_device`: each index of img is named by exactly 4 entries.
All inputs are finite; a program needn't handle non-finite values.
Results may differ from a plain program's by a relative error of at most 0.013.
Values may be sent and summed in bfloat16 or wider, within the bound.
A program may use at most 192 MiB of HBM per device.

v0:
```python
from functools import partial

import jax
import jax.numpy as jnp
from jax import lax
from jax.sharding import PartitionSpec as P

HEADS = 8
HEAD_DIM = 64


epsilon = 1e-05


def layer_norm(values, gain, bias):
    centre = values - jnp.mean(values, axis=-1, keepdims=True)
    variance = jnp.mean(centre * centre, axis=-1, keepdims=True)
    return centre * lax.rsqrt(variance + epsilon) * gain + bias


def project(left, weight):
    return jnp.einsum("crd,de->cre", left, weight, preferred_element_type=jnp.float32)


def project_back(grad, weight):
    return jnp.einsum("cre,de->crd", grad, weight, preferred_element_type=jnp.float32)


def weight_grad(left, grad):
    return jnp.einsum("crd,cre->de", left, grad, preferred_element_type=jnp.float32)


def split_heads(values):
    return values.reshape(values.shape[0], values.shape[1], HEADS, HEAD_DIM)


def local(
    patches,
    latents,
    cotangent,
    doc_images,
    doc_device,
    query_weight,
    key_weight,
    value_weight,
    output_weight,
    up_weight,
    down_weight,
    media_gain,
    media_bias,
    latent_gain,
    latent_bias,
    ffn_gain,
    ffn_bias,
):
    slots = patches.shape[0]
    own_patches = patches.shape[1]
    scale = HEAD_DIM ** (-0.5)
    mine = lax.axis_index("img")
    holding = jnp.sum(jnp.where(doc_device == mine, doc_images, 0))
    active = (jnp.arange(slots, dtype=jnp.int32) < holding).astype(jnp.float32)[:, None, None]
    media = patches.astype(jnp.float32)
    latent = latents.astype(jnp.float32)
    media_norm = layer_norm(media, media_gain, media_bias)
    latent_norm = layer_norm(latent, latent_gain, latent_bias)
    key_rows = jnp.concatenate([media_norm, latent_norm], axis=1).astype(jnp.bfloat16)
    latent_low = key_rows[:, own_patches:]
    keys_low = project(key_rows, key_weight).astype(jnp.bfloat16)
    values_low = project(key_rows, value_weight).astype(jnp.bfloat16)
    keys_all, values_all = (
        lax.all_gather(keys_low, "lat", axis=1, tiled=True),
        lax.all_gather(values_low, "lat", axis=1, tiled=True),
    )
    query_low = (scale * project(latent_low, query_weight)).astype(jnp.bfloat16)
    query_heads = split_heads(query_low)
    scores = jnp.einsum(
        "cqhd,ckhd->chqk", query_heads, split_heads(keys_all), preferred_element_type=jnp.float32
    )
    top = jnp.max(scores, axis=-1, keepdims=True)
    expo = jnp.exp(scores - top)
    total = jnp.sum(expo, axis=-1, keepdims=True)
    log_total = top + jnp.log(total)
    probs_low = (expo / total).astype(jnp.bfloat16)
    attended = jnp.einsum(
        "chqk,ckhd->cqhd", probs_low, split_heads(values_all), preferred_element_type=jnp.float32
    )
    attended_low = attended.reshape(query_low.shape).astype(jnp.bfloat16)
    residual = latent + project(attended_low, output_weight)
    ffn_low = layer_norm(residual, ffn_gain, ffn_bias).astype(jnp.bfloat16)
    pre_act = project(ffn_low, up_weight)
    act_low = jax.nn.gelu(pre_act, approximate=False).astype(jnp.bfloat16)
    new_latents = ((residual + project(act_low, down_weight)) * active).astype(jnp.bfloat16)
    out_grad = (cotangent.astype(jnp.float32) * active).astype(jnp.bfloat16)
    down_grad = weight_grad(act_low, out_grad)
    act_grad = project_back(out_grad, down_weight)
    gelu_back = jax.vjp(partial(jax.nn.gelu, approximate=False), pre_act)[1]
    pre_grad = gelu_back(act_grad)[0].astype(jnp.bfloat16)
    up_grad = weight_grad(ffn_low, pre_grad)
    ffn_in_grad = project_back(pre_grad, up_weight)
    residual_part, ffn_gain_grad, ffn_bias_grad = jax.vjp(layer_norm, residual, ffn_gain, ffn_bias)[
        1
    ](ffn_in_grad)
    residual_grad = out_grad.astype(jnp.float32) + residual_part
    branch_low = residual_grad.astype(jnp.bfloat16)
    output_grad = weight_grad(attended_low, branch_low)
    attended_grad = split_heads(project_back(branch_low, output_weight).astype(jnp.bfloat16))
    keys_back, values_back = (
        lax.all_gather(keys_low, "lat", axis=1, tiled=True),
        lax.all_gather(values_low, "lat", axis=1, tiled=True),
    )
    key_heads = split_heads(keys_back)
    value_heads = split_heads(values_back)
    scores_back = jnp.einsum(
        "cqhd,ckhd->chqk", query_heads, key_heads, preferred_element_type=jnp.float32
    )
    probs = jnp.exp(scores_back - log_total)
    probs_again = probs.astype(jnp.bfloat16)
    prob_grad = jnp.einsum(
        "cqhd,ckhd->chqk", attended_grad, value_heads, preferred_element_type=jnp.float32
    )
    score_grad = (probs * (prob_grad - jnp.sum(prob_grad * probs, axis=-1, keepdims=True))).astype(
        jnp.bfloat16
    )
    values_part = jnp.einsum(
        "chqk,cqhd->ckhd", probs_again, attended_grad, preferred_element_type=jnp.float32
    )
    keys_part = jnp.einsum(
        "chqk,cqhd->ckhd", score_grad, query_heads, preferred_element_type=jnp.float32
    )
    queries_grad = jnp.einsum(
        "chqk,ckhd->cqhd", score_grad, key_heads, preferred_element_type=jnp.float32
    )
    queries_grad = queries_grad.reshape(query_low.shape).astype(jnp.bfloat16)
    keys_grad, values_grad = (
        lax.psum_scatter(
            keys_part.reshape(keys_back.shape), "lat", scatter_dimension=1, tiled=True
        ),
        lax.psum_scatter(
            values_part.reshape(values_back.shape), "lat", scatter_dimension=1, tiled=True
        ),
    )
    keys_grad_low = keys_grad.astype(jnp.bfloat16)
    values_grad_low = values_grad.astype(jnp.bfloat16)
    key_grad = weight_grad(key_rows, keys_grad_low)
    value_grad = weight_grad(key_rows, values_grad_low)
    query_grad = scale * weight_grad(latent_low, queries_grad)
    rows_grad = project_back(keys_grad_low, key_weight) + project_back(
        values_grad_low, value_weight
    )
    latent_norm_grad = rows_grad[:, own_patches:] + scale * project_back(queries_grad, query_weight)
    patches_grad, media_gain_grad, media_bias_grad = jax.vjp(
        layer_norm, media, media_gain, media_bias
    )[1](rows_grad[:, :own_patches])
    latent_part, latent_gain_grad, latent_bias_grad = jax.vjp(
        layer_norm, latent, latent_gain, latent_bias
    )[1](latent_norm_grad)
    latents_grad = residual_grad + latent_part
    summed = (
        lax.psum_scatter(query_grad, ("img", "lat"), scatter_dimension=0, tiled=True),
        lax.psum_scatter(key_grad, ("img", "lat"), scatter_dimension=0, tiled=True),
        lax.psum_scatter(value_grad, ("img", "lat"), scatter_dimension=0, tiled=True),
        lax.psum_scatter(output_grad, ("img", "lat"), scatter_dimension=0, tiled=True),
        lax.psum_scatter(up_grad, ("img", "lat"), scatter_dimension=0, tiled=True),
        lax.psum_scatter(down_grad, ("img", "lat"), scatter_dimension=0, tiled=True),
        lax.psum_scatter(media_gain_grad, ("img", "lat"), scatter_dimension=0, tiled=True),
        lax.psum_scatter(media_bias_grad, ("img", "lat"), scatter_dimension=0, tiled=True),
        lax.psum_scatter(latent_gain_grad, ("img", "lat"), scatter_dimension=0, tiled=True),
        lax.psum_scatter(latent_bias_grad, ("img", "lat"), scatter_dimension=0, tiled=True),
        lax.psum_scatter(ffn_gain_grad, ("img", "lat"), scatter_dimension=0, tiled=True),
        lax.psum_scatter(ffn_bias_grad, ("img", "lat"), scatter_dimension=0, tiled=True),
    )
    return (
        new_latents,
        patches_grad,
        latents_grad,
        summed[0],
        summed[1],
        summed[2],
        summed[3],
        summed[4],
        summed[5],
        summed[6],
        summed[7],
        summed[8],
        summed[9],
        summed[10],
        summed[11],
    )


def solution(mesh):
    placed = (
        P("img", "lat", None),
        P("img", "lat", None),
        P("img", "lat", None),
        P(),
        P(),
        P(),
        P(),
        P(),
        P(),
        P(),
        P(),
        P(),
        P(),
        P(),
        P(),
        P(),
        P(),
    )
    return jax.shard_map(
        local,
        mesh=mesh,
        in_specs=placed,
        out_specs=(
            P("img", "lat", None),
            P("img", "lat", None),
            P("img", "lat", None),
            P(("img", "lat"), None),
            P(("img", "lat"), None),
            P(("img", "lat"), None),
            P(("img", "lat"), None),
            P(("img", "lat"), None),
            P(("img", "lat"), None),
            P(("img", "lat")),
            P(("img", "lat")),
            P(("img", "lat")),
            P(("img", "lat")),
            P(("img", "lat")),
            P(("img", "lat")),
        ),
        check_vma=False,
    )
```

profile of v0, /device:TPU:0, one launch (start us, length us, event | category | flops | bytes accessed | tf_op | source)
XLA Modules:
  0.0 1568.8 jit_solution(2975339634770484307)
XLA Ops:
  17.5 4.6 convolution_convert_fusion.1
  26.6 32.7 %all-gather.5.cloned.1.call-done = bf16[8,320,512]{2,1,0:T(8,128)(2,1)} async-done(((bf16[8,160,512]{2,1,0:T(8,128)(2,1)}), bf16[8,320,512]{2,1,0:T(8,128)(2,1)}) %all-gather.5.cloned.1.call-update) | async-done | bytes 2621456 | tf_op jit(solution)/shard_map/all_gather | solution.py:71
  69.4 31.1 %all-gather.3.cloned.1.call-done = bf16[8,320,512]{2,1,0:T(8,128)(2,1)} async-done(((bf16[8,160,512]{2,1,0:T(8,128)(2,1)}), bf16[8,320,512]{2,1,0:T(8,128)(2,1)}) %all-gather.3.cloned.1.call-update) | async-done | bytes 2621456 | tf_op jit(solution)/shard_map/all_gather | solution.py:72
  113.8 6.9 fusion.69
  120.7 10.3 multiply_convert_fusion
  131.0 7.2 add_convert_fusion
  138.2 6.8 multiply_reduce_fusion.1
  149.1 5.8 fusion.29
  154.9 6.2 copy.60
  170.2 6.3 copy.58
  189.8 37.2 %reduce-scatter.11.cloned.1.call-done = f32[8,160,512]{2,1,0:T(8,128)} async-done(((f32[8,320,512]{2,1,0:T(8,128)}), f32[8,160,512]{2,1,0:T(8,128)}) %reduce-scatter.11.cloned.1.call-update) | async-done | bytes 2621456 | tf_op jit(solution)/shard_map/reduce_scatter | solution.py:138
  227.0 5.5 convolution_bitcast_fusion.3
  232.5 62.4 %reduce-scatter.9.cloned.1.call-done = f32[8,160,512]{2,1,0:T(8,128)} async-done(((f32[8,320,512]{2,1,0:T(8,128)}), f32[8,160,512]{2,1,0:T(8,128)}) %reduce-scatter.9.cloned.1.call-update) | async-done | bytes 2621456 | tf_op jit(solution)/shard_map/reduce_scatter | solution.py:135
  295.0 5.4 convolution_bitcast_fusion.4
  300.5 10.1 convolution_bitcast_fusion.1
  310.9 9.8 convolution_bitcast_fusion
  320.7 7.5 fusion.45
  337.4 40.1 %all-reduce.6 = (f32[1024]{0:T(1024)S(1)}, f32[1024]{0:T(1024)S(1)}, f32[1024]{0:T(1024)S(1)}, f32[1024]{0:T(1024)S(1)}, f32[1024]{0:T(1024)S(1)}, /*index=5*/f32[1024]{0:T(1024)S(1)}) all-reduce(f32[1024]{0:T(1024)S(1)} %get-tuple-element.15, ...), channel_id=10, replica_groups=mesh['img'=16,'lat'=2] {'img','lat'}, use_global_device_ids=true, to_apply=%region_25.26.clone | all-reduce | flops 6144 | bytes 49152
  388.6 46.5 %reduce-scatter.19.cloned.1.call-done = f32[16,1024]{1,0:T(8,128)} async-done(((f32[512,1024]{1,0:T(8,128)}), f32[16,1024]{1,0:T(8,128)}) %reduce-scatter.19.cloned.1.call-update) | async-done | bytes 65552 | tf_op jit(solution)/shard_map/reduce_scatter | solution.py:162
  435.2 136.3 %reduce-scatter.13.cloned.1.call-done = f32[32,512]{1,0:T(8,128)} async-done(((f32[1024,512]{1,0:T(8,128)}), f32[32,512]{1,0:T(8,128)}) %reduce-scatter.13.cloned.1.call-update) | async-done | bytes 65552 | tf_op jit(solution)/shard_map/reduce_scatter | solution.py:159
  571.5 136.4 %reduce-scatter.17.cloned.1.call-done = f32[32,512]{1,0:T(8,128)} async-done(((f32[1024,512]{1,0:T(8,128)}), f32[32,512]{1,0:T(8,128)}) %reduce-scatter.17.cloned.1.call-update) | async-done | bytes 65552 | tf_op jit(solution)/shard_map/reduce_scatter | solution.py:161
  707.9 136.3 %reduce-scatter.15.cloned.1.call-done = f32[32,512]{1,0:T(8,128)} async-done(((f32[1024,512]{1,0:T(8,128)}), f32[32,512]{1,0:T(8,128)}) %reduce-scatter.15.cloned.1.call-update) | async-done | bytes 65552 | tf_op jit(solution)/shard_map/reduce_scatter | solution.py:160
  844.2 356.1 %reduce-scatter.21.cloned.1.call-done = f32[32,4096]{1,0:T(8,128)} async-done(((f32[1024,4096]{1,0:T(8,128)}), f32[32,4096]{1,0:T(8,128)}) %reduce-scatter.21.cloned.1.call-update) | async-done | bytes 524304 | tf_op jit(solution)/shard_map/reduce_scatter | solution.py:163
  1200.3 361.4 %reduce-scatter.23.cloned.1.call-done = f32[128,1024]{1,0:T(8,128)} async-done(((f32[4096,1024]{1,0:T(8,128)}), f32[128,1024]{1,0:T(8,128)}) %reduce-scatter.23.cloned.1.call-update) | async-done | bytes 524304 | tf_op jit(solution)/shard_map/reduce_scatter | solution.py:164
  (143 shorter events, 84.8 us)
Async XLA Ops:
  7.2 7.6 copy-start
  7.2 5.3 copy-start.3
  7.2 5.0 copy-start.23
  7.2 5.0 copy-start.25
  7.2 5.3 copy-start.24
  7.2 5.3 copy-start.27
  7.2 52.0 %all-gather.5.cloned.1.call-start = ((), (), s32[]{:S(2)}) async-start(), calls=%async_computation.9 | async-start | bytes 3932160 | tf_op jit(solution)/shard_map/all_gather | solution.py:71
  17.4 7.9 copy-start.28
  17.4 7.9 copy-start.29
  17.4 83.0 %all-gather.3.cloned.1.call-start = ((), (), s32[]{:S(2)}) async-start(), calls=%async_computation.8 | async-start | bytes 3932160 | tf_op jit(solution)/shard_map/all_gather | solution.py:72
  22.1 204.9 %reduce-scatter.11.cloned.1.call-start = ((), (), s32[]{:S(2)}) async-start(), calls=%async_computation.11 | async-start | bytes 7864320 | tf_op jit(solution)/shard_map/reduce_scatter | solution.py:138
  109.1 4.7 copy-start.26
  111.5 9.2 copy-start.20
  113.5 31.6 %copy-start.9 = (f32[8,32,1024]{2,1,0:T(8,128)}, f32[8,32,1024]{2,1,0:T(8,128)S(1)}, u32[]{:S(2)}) copy-start(f32[8,32,1024]{2,1,0:T(8,128)S(1)} %get-tuple-element.40) | copy-start | bytes 3145732
  120.7 10.3 copy-start.15
  138.2 6.8 copy-start.31
  161.2 133.8 %reduce-scatter.9.cloned.1.call-start = ((), (), s32[]{:S(2)}) async-start(), calls=%async_computation.10 | async-start | bytes 7864320 | tf_op jit(solution)/shard_map/reduce_scatter | solution.py:135
  176.5 258.6 %reduce-scatter.19.cloned.1.call-start = ((), (), s32[]{:S(2)}) async-start(), calls=%async_computation.15 | async-start | bytes 2162688 | tf_op jit(solution)/shard_map/reduce_scatter | solution.py:162
  180.4 391.1 %reduce-scatter.13.cloned.1.call-start = ((), (), s32[]{:S(2)}) async-start(), calls=%async_computation.12 | async-start | bytes 2162688 | tf_op jit(solution)/shard_map/reduce_scatter | solution.py:159
  189.8 518.1 %reduce-scatter.17.cloned.1.call-start = ((), (), s32[]{:S(2)}) async-start(), calls=%async_computation.14 | async-start | bytes 2162688 | tf_op jit(solution)/shard_map/reduce_scatter | solution.py:161
  232.5 611.7 %reduce-scatter.15.cloned.1.call-start = ((), (), s32[]{:S(2)}) async-start(), calls=%async_computation.13 | async-start | bytes 2162688 | tf_op jit(solution)/shard_map/reduce_scatter | solution.py:160
  300.4 899.9 %reduce-scatter.21.cloned.1.call-start = ((), (), s32[]{:S(2)}) async-start(), calls=%async_computation.16 | async-start | bytes 17301504 | tf_op jit(solution)/shard_map/reduce_scatter | solution.py:163
  310.6 1251.1 %reduce-scatter.23.cloned.1.call-start = ((), (), s32[]{:S(2)}) async-start(), calls=%async_computation.17 | async-start | bytes 17301504 | tf_op jit(solution)/shard_map/reduce_scatter | solution.py:164
  320.7 7.5 copy-start.14
  (18 other events, 39.0 us)
Sparse Core Ops, SparseCore 0:
  17.5 41.7 all-gather.4
  61.4 39.0 all-gather.2
  161.3 65.6 reduce-scatter.10
  229.3 65.6 reduce-scatter.8
  297.6 137.4 reduce-scatter.18
  438.0 133.5 reduce-scatter.12
  574.4 133.4 reduce-scatter.16
  710.8 133.3 reduce-scatter.14
  847.1 353.2 reduce-scatter.20
  1203.1 358.6 reduce-scatter.22
where the time goes:
time: 1570 us
  waiting for transfers between devices  1340 us (85%)
  matrix products  105 us (7%)
  blocking collectives  40.1 us (3%)
  local copies, waits for them, and re-layouts  39.9 us (3%)
  other arithmetic  31.4 us (2%)
    reduce_scatter x1, waiting for transfers between devices, local(): lax.psum_scatter(down_grad, ('img', 'lat'), scatter_dimension=0, tiled=True)  361 us
    reduce_scatter x1, waiting for transfers between devices, local(): lax.psum_scatter(up_grad, ('img', 'lat'), scatter_dimension=0, tiled=True)  356 us
    reduce_scatter x1, waiting for transfers between devices, local(): lax.psum_scatter(value_grad, ('img', 'lat'), scatter_dimension=0, tiled=T...  136 us
    reduce_scatter x1, waiting for transfers between devices, local(): lax.psum_scatter(query_grad, ('img', 'lat'), scatter_dimension=0, tiled=T...  136 us
    reduce_scatter x1, waiting for transfers between devices, local(): lax.psum_scatter(key_grad, ('img', 'lat'), scatter_dimension=0, tiled=True)  136 us
    reduce_scatter x1, waiting for transfers between devices, local(): lax.psum_scatter(keys_part.reshape(keys_back.shape), 'lat', scatter_dimen...  62.4 us
    reduce_scatter x1, waiting for transfers between devices, local(): lax.psum_scatter(output_grad, ('img', 'lat'), scatter_dimension=0, tiled=...  46.5 us
    unnamed x1, blocking collectives  40.1 us
  transfers between devices with their start and end apart: 10, of which 10 were waited for; matrix products, arithmetic and copies ran while one was open for 6% of the time, Pallas kernels for 0%

commit v1 on v0

v1 whole, which is shorter than its diff:
```python
from functools import partial

import jax
import jax.numpy as jnp
from jax import lax
from jax.experimental import pallas as pl
from jax.experimental.pallas import tpu as pltpu
from jax.sharding import PartitionSpec as P

HEADS = 8
HEAD_DIM = 64
INNER = HEADS * HEAD_DIM
LANES = 128
PER = LANES // HEADS
EPS = 1e-05
BF = jnp.bfloat16
F32 = jnp.float32
VMEM_LIMIT = 56 * 1024 * 1024


def dot(a, b):
    return lax.dot_general(a, b, (((1,), (0,)), ((), ())), preferred_element_type=F32)


def dot_t(a, b):
    return lax.dot_general(a, b, (((1,), (1,)), ((), ())), preferred_element_type=F32)


def t_dot(a, b):
    return lax.dot_general(a, b, (((0,), (0,)), ((), ())), preferred_element_type=F32)


def call(body, grid, ins, outs, args, flops, scratch=()):
    moved = sum(a.size * a.dtype.itemsize for a in args)
    moved += sum(o[0].size * o[0].dtype.itemsize for o in outs)
    return pl.pallas_call(
        body,
        grid=grid,
        in_specs=ins,
        out_specs=[o[1] for o in outs],
        out_shape=[o[0] for o in outs],
        scratch_shapes=list(scratch),
        compiler_params=pltpu.CompilerParams(
            dimension_semantics=("arbitrary",) * len(grid), vmem_limit_bytes=VMEM_LIMIT
        ),
        cost_estimate=pl.CostEstimate(flops=flops, bytes_accessed=moved, transcendentals=0),
    )(*args)


def whole(shape):
    return pl.BlockSpec(shape, lambda *_: (0,) * len(shape))


def rows(block, width):
    return pl.BlockSpec((block, width), lambda i: (i, 0))


def cols(height, block):
    return pl.BlockSpec((height, block), lambda i: (0, i))


def struct(shape, dtype):
    return jax.ShapeDtypeStruct(shape, dtype)


def centred(v):
    centre = v - jnp.mean(v, axis=-1, keepdims=True)
    scale = lax.rsqrt(jnp.mean(centre * centre, axis=-1, keepdims=True) + EPS)
    return centre * scale, scale


def norm_back(unit, scale, gain, grad):
    push = grad * gain
    mean_push = jnp.mean(push, axis=-1, keepdims=True)
    mean_both = jnp.mean(push * unit, axis=-1, keepdims=True)
    return scale * (push - mean_push - unit * mean_both)


def column_sum(v):
    return jnp.sum(v, axis=0, keepdims=True)


def latent_body(latent, gain, bias, wq, norm, query):
    unit, _ = centred(latent[...].astype(F32))
    low = (unit * gain[...] + bias[...]).astype(BF)
    norm[...] = low
    query[...] = (HEAD_DIM**-0.5 * dot(low, wq[...])).astype(BF)


def media_body(patch, gain, bias, wk, wv, latent_norm, norm, kp, vp, kl, vl):
    @pl.when(pl.program_id(0) == 0)
    def _():
        kl[...] = dot(latent_norm[...], wk[...]).astype(BF)
        vl[...] = dot(latent_norm[...], wv[...]).astype(BF)

    unit, _ = centred(patch[...].astype(F32))
    low = (unit * gain[...] + bias[...]).astype(BF)
    norm[...] = low
    kp[...] = dot(low, wk[...]).astype(BF)
    vp[...] = dot(low, wv[...]).astype(BF)


def head_of(shape):
    return lax.broadcasted_iota(jnp.int32, shape, 1) // HEAD_DIM


def spread_rows(v):
    head = head_of(v.shape)
    zero = jnp.zeros_like(v)
    return jnp.concatenate([jnp.where(head == h, v, zero) for h in range(HEADS)], axis=0)


def gather_rows(v):
    count = v.shape[0] // HEADS
    head = head_of((count, v.shape[1]))
    total = jnp.zeros((count, v.shape[1]), F32)
    for h in range(HEADS):
        total = jnp.where(head == h, v[h * count : (h + 1) * count], total)
    return total


def pack_lanes(columns):
    count = columns[0].shape[0]
    lane = lax.broadcasted_iota(jnp.int32, (count, LANES), 1)
    step = LANES // len(columns)
    total = jnp.zeros((count, LANES), F32)
    for h, column in enumerate(columns):
        total = jnp.where(lane // step == h, column, total)
    return total


def widen(packed):
    head = head_of((packed.shape[0], INNER))
    total = jnp.zeros((packed.shape[0], INNER), F32)
    for h in range(HEADS):
        total = jnp.where(head == h, packed[:, h * PER : h * PER + 1], total)
    return total


def stack_heads(packed, offset):
    return jnp.concatenate(
        [packed[:, h * PER + offset : h * PER + offset + 1] for h in range(HEADS)], axis=0
    )


def attend_body(qo, qp, kp, vp, kl, vl, oo, op, so, sp):
    own = qo.shape[0]
    big = spread_rows(jnp.concatenate([qo[...], qp[...]], axis=0))
    keys = jnp.concatenate([kp[...], kl[...]], axis=0)
    values = jnp.concatenate([vp[...], vl[...]], axis=0)
    scores = dot_t(big, keys)
    top = jnp.max(scores, axis=-1, keepdims=True)
    expo = jnp.exp(scores - top)
    total = jnp.sum(expo, axis=-1, keepdims=True)
    probs = (expo / total).astype(BF)
    out = gather_rows(dot(probs, values))
    log_total = top + jnp.log(total)
    count = log_total.shape[0] // HEADS
    packed = pack_lanes([log_total[h * count : (h + 1) * count] for h in range(HEADS)])
    oo[...] = out[:own]
    op[...] = out[own:].astype(BF)
    so[...] = packed[:own]
    sp[...] = packed[own:]


def forward_body(
    slot_rows,
    holding,
    oo,
    orecv,
    so,
    srecv,
    latent,
    cot,
    wo,
    wup,
    wdown,
    gain,
    bias,
    new_latents,
    act_out,
    pre_out,
    ffn_t,
    og_out,
    residual_grad,
    attended_grad,
    stats,
    output_grad,
    vectors,
    residual,
    ffn_in,
    acc,
    gacc,
    attended,
    packed,
):
    step = pl.program_id(0)
    count = latent.shape[0]
    slot = lax.broadcasted_iota(jnp.int32, (count, 1), 0) // slot_rows
    live = jnp.where(slot < holding[0, 0], 1.0, 0.0).astype(F32)

    @pl.when(step == 0)
    def _():
        a, b = so[...], srecv[...]
        top = jnp.maximum(a, b)
        both = top + jnp.log(jnp.exp(a - top) + jnp.exp(b - top))
        packed[...] = both
        mix = widen(jnp.exp(a - both)) * oo[...]
        mix += widen(jnp.exp(b - both)) * orecv[...].astype(F32)
        attended[...] = mix
        res = latent[...].astype(F32) + dot(mix.astype(BF), wo[...])
        residual[...] = res
        unit, _ = centred(res)
        low = (unit * gain[...] + bias[...]).astype(BF)
        ffn_in[...] = low
        ffn_t[...] = low.T
        og_out[...] = (cot[...].astype(F32) * live).astype(BF)
        acc[...] = jnp.zeros_like(acc)
        gacc[...] = jnp.zeros_like(gacc)

    pre = dot(ffn_in[...], wup[...])
    cdf = 0.5 * (1.0 + lax.erf(pre * (0.5**0.5)))
    act = (pre * cdf).astype(BF)
    act_out[...] = act
    acc[...] += dot(act, wdown[...])
    act_grad = dot_t(og_out[...], wdown[...])
    pdf = jnp.exp(-0.5 * pre * pre) * 0.3989422804014327
    pre_grad = (act_grad * (cdf + pre * pdf)).astype(BF)
    pre_out[...] = pre_grad
    gacc[...] += dot_t(pre_grad, wup[...])

    @pl.when(step == pl.num_programs(0) - 1)
    def _():
        res = residual[...]
        new_latents[...] = ((res + acc[...]) * live).astype(BF)
        unit, scale = centred(res)
        grad = gacc[...]
        vectors[0:1, :] = column_sum(grad * unit)
        vectors[1:2, :] = column_sum(grad)
        res_grad = og_out[...].astype(F32) + norm_back(unit, scale, gain[...], grad)
        residual_grad[...] = res_grad
        branch = res_grad.astype(BF)
        back = dot_t(branch, wo[...]).astype(BF)
        attended_grad[...] = back
        mix = attended[...]
        product = back.astype(F32) * mix
        head = head_of(product.shape)
        sums = [
            jnp.sum(jnp.where(head == h, product, 0.0), axis=-1, keepdims=True)
            for h in range(HEADS)
        ]
        delta = pack_lanes(sums)
        lane = lax.broadcasted_iota(jnp.int32, delta.shape, 1)
        stats[...] = jnp.where(lane % PER < PER // 2, packed[...], delta)
        output_grad[...] = t_dot(mix.astype(BF), branch).astype(BF)


def attend_back_body(qo, qp, kp, vp, kl, vl, do, dp, so, sp, dkvp, dkvl, dqo, dqp):
    own = qo.shape[0]
    patches = kp.shape[0]
    big = spread_rows(jnp.concatenate([qo[...], qp[...]], axis=0))
    back = spread_rows(jnp.concatenate([do[...], dp[...]], axis=0))
    keys = jnp.concatenate([kp[...], kl[...]], axis=0)
    values = jnp.concatenate([vp[...], vl[...]], axis=0)
    stats = jnp.concatenate([so[...], sp[...]], axis=0)
    probs = jnp.exp(dot_t(big, keys) - stack_heads(stats, 0))
    score_grad = (probs * (dot_t(back, values) - stack_heads(stats, PER // 2))).astype(BF)
    values_grad = t_dot(probs.astype(BF), back).astype(BF)
    keys_grad = t_dot(score_grad, big).astype(BF)
    dkvp[:, :INNER] = keys_grad[:patches]
    dkvp[:, INNER:] = values_grad[:patches]
    dkvl[:, :INNER] = keys_grad[patches:]
    dkvl[:, INNER:] = values_grad[patches:]
    dq = gather_rows(dot(score_grad, keys))
    dqo[...] = dq[:own]
    dqp[...] = dq[own:].astype(BF)


def up_grad_body(left, right, out):
    out[...] = dot(left[...], right[...]).astype(BF)


def down_grad_body(left, right, out):
    out[...] = t_dot(left[...], right[...]).astype(BF)


def kv_grad_body(media, latent, dkvp, dkvl, out):
    out[...] = (t_dot(media[...], dkvp[...]) + t_dot(latent[...], dkvl[...])).astype(BF)


def patch_back_body(patch, dkvp, wk, wv, gain, out, vectors):
    @pl.when(pl.program_id(0) == 0)
    def _():
        vectors[...] = jnp.zeros_like(vectors)

    grad = dot_t(dkvp[:, :INNER], wk[...]) + dot_t(dkvp[:, INNER:], wv[...])
    unit, scale = centred(patch[...].astype(F32))
    vectors[0:1, :] += column_sum(grad * unit)
    vectors[1:2, :] += column_sum(grad)
    out[...] = norm_back(unit, scale, gain[...], grad)


def latent_back_body(
    latent, norm, dkvl, dqo, drecv, residual_grad, wq, wk, wv, gain, out, query_grad, vectors
):
    dq = (dqo[...] + drecv[...].astype(F32)).astype(BF)
    query_grad[...] = (HEAD_DIM**-0.5 * t_dot(norm[...], dq)).astype(BF)
    grad = dot_t(dkvl[:, :INNER], wk[...]) + dot_t(dkvl[:, INNER:], wv[...])
    grad += HEAD_DIM**-0.5 * dot_t(dq, wq[...])
    unit, scale = centred(latent[...].astype(F32))
    vectors[0:1, :] = column_sum(grad * unit)
    vectors[1:2, :] = column_sum(grad)
    out[...] = residual_grad[...] + norm_back(unit, scale, gain[...], grad)


def swap_lat(v):
    return lax.ppermute(v, "lat", [(0, 1), (1, 0)])


def halving_sum(v, order, bits, count, keep):
    left = list(range(bits - 1, -1, -1)) + [-1]
    mine = lax.axis_index("img")
    for place, axis in enumerate(order):
        dim = left.index(axis)
        if axis < 0:
            bit = lax.axis_index("lat")
            pairs, name = [(0, 1), (1, 0)], "lat"
        else:
            bit = (mine // 2**axis) % 2
            pairs, name = [(i, i ^ 2**axis) for i in range(count)], "img"
        out = lax.dynamic_index_in_dim(v, 1 - bit, dim, keepdims=False)
        stay = lax.dynamic_index_in_dim(v, bit, dim, keepdims=False)
        got = lax.ppermute(out, name, pairs)
        v = stay.astype(F32) + got.astype(F32)
        if place < len(order) - 1 and keep == BF:
            v = v.astype(BF)
        left.pop(dim)
    return v


def local(
    count,
    patches,
    latents,
    cotangent,
    doc_images,
    doc_device,
    query_weight,
    key_weight,
    value_weight,
    output_weight,
    up_weight,
    down_weight,
    media_gain,
    media_bias,
    latent_gain,
    latent_bias,
    ffn_gain,
    ffn_bias,
):
    slots, own_patches, width = patches.shape
    own_latents = latents.shape[1]
    hidden = up_weight.shape[1]
    np_, nl = slots * own_patches, slots * own_latents
    mine = lax.axis_index("img")
    holding = jnp.sum(jnp.where(doc_device == mine, doc_images, 0)).reshape(1, 1)
    patch = patches.reshape(np_, width)
    latent = latents.reshape(nl, width)
    cot = cotangent.reshape(nl, width)
    mg, mb = media_gain.reshape(1, width), media_bias.reshape(1, width)
    lg, lb = latent_gain.reshape(1, width), latent_bias.reshape(1, width)
    fg, fb = ffn_gain.reshape(1, width), ffn_bias.reshape(1, width)
    wspec = whole((width, INNER))
    vspec = whole((1, width))
    lspec = whole((nl, width))

    norm_l, query = call(
        latent_body,
        (1,),
        [lspec, vspec, vspec, wspec],
        [(struct((nl, width), BF), lspec), (struct((nl, INNER), BF), whole((nl, INNER)))],
        (latent, lg, lb, query_weight),
        2 * nl * width * INNER,
    )
    query_peer = swap_lat(query)
    blk = min(np_, 256)
    norm_m, kp, vp, kl, vl = call(
        media_body,
        (np_ // blk,),
        [rows(blk, width), vspec, vspec, wspec, wspec, lspec],
        [
            (struct((np_, width), BF), rows(blk, width)),
            (struct((np_, INNER), BF), rows(blk, INNER)),
            (struct((np_, INNER), BF), rows(blk, INNER)),
            (struct((nl, INNER), BF), whole((nl, INNER))),
            (struct((nl, INNER), BF), whole((nl, INNER))),
        ],
        (patch, mg, mb, key_weight, value_weight, norm_l),
        4 * (np_ + nl) * width * INNER,
    )
    q_s, p_s, s_s = rows(own_latents, INNER), rows(own_patches, INNER), rows(own_latents, LANES)
    att_flops = 4 * slots * (own_patches + own_latents) * INNER * INNER
    o_own, o_peer, s_own, s_peer = call(
        attend_body,
        (slots,),
        [q_s, q_s, p_s, p_s, q_s, q_s],
        [
            (struct((nl, INNER), F32), q_s),
            (struct((nl, INNER), BF), q_s),
            (struct((nl, LANES), F32), s_s),
            (struct((nl, LANES), F32), s_s),
        ],
        (query, query_peer, kp, vp, kl, vl),
        att_flops,
    )
    o_recv, s_recv = swap_lat(o_peer), swap_lat(s_peer)
    fblk = min(hidden, 512)
    nspec = whole((nl, INNER))
    (
        new_latents,
        act,
        pre_grad,
        ffn_t,
        out_grad,
        residual_grad,
        attended_grad,
        stats,
        output_grad,
        ffn_vec,
    ) = call(
        partial(forward_body, own_latents),
        (hidden // fblk,),
        [
            pl.BlockSpec(memory_space=pltpu.SMEM),
            nspec,
            nspec,
            whole((nl, LANES)),
            whole((nl, LANES)),
            lspec,
            lspec,
            whole((INNER, width)),
            cols(width, fblk),
            rows(fblk, width),
            vspec,
            vspec,
        ],
        [
            (struct((nl, width), BF), lspec),
            (struct((nl, hidden), BF), cols(nl, fblk)),
            (struct((nl, hidden), BF), cols(nl, fblk)),
            (struct((width, nl), BF), whole((width, nl))),
            (struct((nl, width), BF), lspec),
            (struct((nl, width), F32), lspec),
            (struct((nl, INNER), BF), nspec),
            (struct((nl, LANES), F32), whole((nl, LANES))),
            (struct((INNER, width), BF), whole((INNER, width))),
            (struct((2, width), F32), whole((2, width))),
        ],
        (
            holding,
            o_own,
            o_recv,
            s_own,
            s_recv,
            latent,
            cot,
            output_weight,
            up_weight,
            down_weight,
            fg,
            fb,
        ),
        8 * nl * width * hidden,
        scratch=[
            pltpu.VMEM((nl, width), F32),
            pltpu.VMEM((nl, width), BF),
            pltpu.VMEM((nl, width), F32),
            pltpu.VMEM((nl, width), F32),
            pltpu.VMEM((nl, INNER), F32),
            pltpu.VMEM((nl, LANES), F32),
        ],
    )
    grad_peer, stats_peer = swap_lat(attended_grad), swap_lat(stats)
    (down_grad,) = call(
        down_grad_body,
        (hidden // fblk,),
        [cols(nl, fblk), lspec],
        [(struct((hidden, width), BF), rows(fblk, width))],
        (act, out_grad),
        2 * nl * width * hidden,
    )
    (up_grad,) = call(
        up_grad_body,
        (hidden // fblk,),
        [whole((width, nl)), cols(nl, fblk)],
        [(struct((width, hidden), BF), cols(width, fblk))],
        (ffn_t, pre_grad),
        2 * nl * width * hidden,
    )
    dkvp, dkvl, dq_own, dq_peer = call(
        attend_back_body,
        (slots,),
        [q_s, q_s, p_s, p_s, q_s, q_s, q_s, q_s, s_s, s_s],
        [
            (struct((np_, 2 * INNER), BF), rows(own_patches, 2 * INNER)),
            (struct((nl, 2 * INNER), BF), rows(own_latents, 2 * INNER)),
            (struct((nl, INNER), F32), q_s),
            (struct((nl, INNER), BF), q_s),
        ],
        (query, query_peer, kp, vp, kl, vl, attended_grad, grad_peer, stats, stats_peer),
        att_flops * 5 // 2,
    )
    dq_recv = swap_lat(dq_peer)
    kblk = 256
    (kv_grad,) = call(
        kv_grad_body,
        (2 * INNER // kblk,),
        [whole((np_, width)), lspec, cols(np_, kblk), cols(nl, kblk)],
        [(struct((width, 2 * INNER), BF), cols(width, kblk))],
        (norm_m, norm_l, dkvp, dkvl),
        4 * (np_ + nl) * width * INNER,
    )
    patches_grad, media_vec = call(
        patch_back_body,
        (np_ // blk,),
        [rows(blk, width), rows(blk, 2 * INNER), wspec, wspec, vspec],
        [(struct((np_, width), F32), rows(blk, width)), (struct((2, width), F32), whole((2, width)))],
        (patch, dkvp, key_weight, value_weight, mg),
        4 * np_ * width * INNER,
    )
    latents_grad, query_grad, latent_vec = call(
        latent_back_body,
        (1,),
        [
            lspec,
            lspec,
            whole((nl, 2 * INNER)),
            nspec,
            nspec,
            lspec,
            wspec,
            wspec,
            wspec,
            vspec,
        ],
        [
            (struct((nl, width), F32), lspec),
            (struct((width, INNER), BF), wspec),
            (struct((2, width), F32), whole((2, width))),
        ],
        (
            latent,
            norm_l,
            dkvl,
            dq_own,
            dq_recv,
            residual_grad,
            query_weight,
            key_weight,
            value_weight,
            lg,
        ),
        8 * nl * width * INNER,
    )

    bits = count.bit_length() - 1
    first = list(range(1, bits))
    orders = (
        [0, -1] + first,
        [0] + first + [-1],
        [0] + first[1:] + [-1] + first[:1],
    )

    def reduce(v, order, keep=BF):
        shape = (2,) * (bits + 1) + (v.shape[0] // (2 * count),) + v.shape[1:]
        return halving_sum(v.reshape(shape), order, bits, count, keep)

    def reduce_parts(v):
        unit = v.shape[1] // 8
        cuts = (0, 3 * unit, 6 * unit, 8 * unit)
        return jnp.concatenate(
            [reduce(v[:, a:b], order) for a, b, order in zip(cuts, cuts[1:], orders)], axis=1
        )

    down_sum = reduce_parts(down_grad)
    up_sum = reduce_parts(up_grad)
    output_sum = reduce(output_grad, orders[1])
    kv_sum = reduce_parts(kv_grad)
    query_sum = reduce(query_grad, orders[0])
    vec = jnp.concatenate([media_vec, latent_vec, ffn_vec], axis=0)
    vec = vec.reshape(6, 2 * count, width // (2 * count)).transpose(1, 0, 2)
    vec_sum = reduce(vec, orders[2], F32)[0]
    return (
        new_latents.reshape(latents.shape),
        patches_grad.reshape(patches.shape),
        latents_grad.reshape(latents.shape),
        query_sum,
        kv_sum[:, :INNER],
        kv_sum[:, INNER:],
        output_sum,
        up_sum,
        down_sum,
        vec_sum[0],
        vec_sum[1],
        vec_sum[2],
        vec_sum[3],
        vec_sum[4],
        vec_sum[5],
    )


def solution(mesh):
    split = P("img", "lat", None)
    both = P(("img", "lat"), None)
    line = P(("img", "lat"))
    return jax.shard_map(
        partial(local, mesh.shape["img"]),
        mesh=mesh,
        in_specs=(split,) * 3 + (P(),) * 14,
        out_specs=(split,) * 3 + (both,) * 6 + (line,) * 6,
        check_vma=False,
    )
```

time: 1570 us -> 391 us (0.25)
  waiting for transfers between devices: 1340 us -> 175 us
  matrix products: 105 us -> 0 us
  Pallas kernels: 0 us -> 88.8 us
  starting transfers between devices: 1.26 us -> 70.6 us
  blocking collectives: 40.1 us -> 0 us
    reduce_scatter x8 -> x0, waiting for transfers between devices: 1270 us -> none  [the longest x1 361 us: local(): lax.psum_scatter(down_grad, ('img', 'lat'), scatter_dimension=0, tiled=True)]
    ppermute x0 -> x66, waiting for transfers between devices: none -> 175 us  [the longest x60 167 us: halving_sum(): got = lax.ppermute(out, name, pairs)]
    dot_general x24 -> x0, matrix products: 105 us -> none  [the longest x6 36.7 us: weight_grad(): jnp.einsum('crd,cre->de', left, grad, preferred_element_type=jnp.float32)]
    pallas_call x0 -> x10, Pallas kernels: none -> 88.8 us  [call(): pl.pallas_call(body, grid=grid, in_specs=ins, out_specs=[o[1] for o in ou...]
    ppermute x0 -> x66, starting transfers between devices: none -> 70.6 us  [the longest x60 63.1 us: halving_sum(): got = lax.ppermute(out, name, pairs)]
    all_gather x2 -> x0, waiting for transfers between devices: 63.8 us -> none  [the longest x1 32.7 us: local(): lax.all_gather(keys_low, 'lat', axis=1, tiled=True)]
    unnamed x1 -> x0, blocking collectives: 40.1 us -> none
    dynamic_slice x0 -> x22, local copies, waits for them, and re-layouts: none -> 19.9 us  [the longest x12 10.7 us: halving_sum(): out = lax.dynamic_index_in_dim(v, 1 - bit, dim, keepdims=False)]
  transfers between devices with their start and end apart: 10 -> 66, of which waited for: 10 -> 36; matrix products, arithmetic and copies ran while one was open for 6% -> 11% of each run, Pallas kernels for 0% -> 10%
where the time goes in v1:
time: 391 us; the launch traced here: 389 us
  waiting for transfers between devices  175 us (45%)
  Pallas kernels  88.8 us (23%)
  starting transfers between devices  70.6 us (18%)
  local copies, waits for them, and re-layouts  35.5 us (9%)
  other arithmetic  17.7 us (5%)
    ppermute x60, waiting for transfers between devices, halving_sum(): got = lax.ppermute(out, name, pairs)  167 us
    pallas_call x10, Pallas kernels, call(): pl.pallas_call(body, grid=grid, in_specs=ins, out_specs=[o[1] for o in ou...  88.8 us
    ppermute x60, starting transfers between devices, halving_sum(): got = lax.ppermute(out, name, pairs)  63.1 us
    convert_element_type x44, other arithmetic, halving_sum(): v = v.astype(BF)  12 us
    dynamic_slice x12, local copies, waits for them, and re-layouts, halving_sum(): out = lax.dynamic_index_in_dim(v, 1 - bit, dim, keepdims=False)  10.7 us
    slice x9, local copies, waits for them, and re-layouts, reduce_parts(): v[:, a:b]  9.46 us
    dynamic_slice x10, local copies, waits for them, and re-layouts, halving_sum(): stay = lax.dynamic_index_in_dim(v, bit, dim, keepdims=False)  9.21 us
    ppermute x6, waiting for transfers between devices, swap_lat(): return lax.ppermute(v, 'lat', [(0, 1), (1, 0)])  8.12 us
  transfers between devices with their start and end apart: 66, of which 36 were waited for; matrix products, arithmetic and copies ran while one was open for 11% of the time, Pallas kernels for 10%

profile of v1, /device:TPU:0, one launch (start us, length us, event | category | flops | bytes accessed | tf_op | source)
XLA Modules:
  0.0 389.0 jit_solution(11891345514961326164)
XLA Ops:
  6.4 7.6 %shard_map.281 = (bf16[1024,1024]{1,0:T(8,128)(2,1)}, bf16[1024,512]{1,0:T(8,128)(2,1)}, bf16[1024,512]{1,0:T(8,128)(2,1)}, bf16[256,512]{1,0:T(8,128)(2,1)}, bf16[256,512]{1,0:T(8,128)(2,1)}) custom-call(bf16[1024,1024]{1,0:T(8,128)(2,1)} %bitcast.409, f32[1,1024]{1,0:T(1,128)} %bitcast.416, f32[1,1024]{1,0:T(1,128)} %bitcast.413, bf16[1024,512]{1,0:T(8,128)(2,1)} %wk.5, ...), custom_call_target="tpu_custom_call" | custom-call | flops 2684354560 | bytes 9445376 | tf_op jit(solution)/shard_map/pallas_call | solution.py:36
  14.8 9.6 %shard_map.282 = (f32[256,512]{1,0:T(8,128)}, bf16[256,512]{1,0:T(8,128)(2,1)}, f32[256,128]{1,0:T(8,128)}, f32[256,128]{1,0:T(8,128)}) custom-call(bf16[256,512]{1,0:T(8,128)(2,1)} %get-tuple-element.45.qo, bf16[256,512]{1,0:T(8,128)(2,1)} %copy-done.18, bf16[1024,512]{1,0:T(8,128)(2,1)} %get-tuple-element.47.kp, bf16[1024,512]{1,0:T(8,128)(2,1)} %get-tuple-element.48.vp, ...), custom_call_target="tpu_custom_call" | custom-call | flops 1342177280 | bytes 4194304 | tf_op jit(solution)/shard_map/pallas_call | solution.py:36
  27.1 8.1 %collective-permute-done.2.srecv = f32[256,128]{1,0:T(8,128)S(1)} collective-permute-done((f32[256,128]{1,0:T(8,128)}, f32[256,128]{1,0:T(8,128)S(1)}, u32[]{:S(2)}, u32[]{:S(2)}) %collective-permute-start.2) | collective-permute-done | bytes 131104 | tf_op jit(solution)/shard_map/ppermute | solution.py:317
  36.0 21.4 %shard_map.283 = (bf16[256,1024]{1,0:T(8,128)(2,1)}, bf16[256,4096]{1,0:T(8,128)(2,1)}, bf16[256,4096]{1,0:T(8,128)(2,1)}, bf16[1024,256]{1,0:T(8,128)(2,1)}, bf...) custom-call(s32[1,1]{1,0:T(1,128)} %bitcast.holding, ...), custom_call_target="tpu_custom_call" | custom-call | flops 8589934592 | bytes 28196868 | tf_op jit(solution)/shard_map/pallas_call | solution.py:36
  57.4 8.4 %shard_map.288 = bf16[1024,4096]{1,0:T(8,128)(2,1)} custom-call(bf16[1024,256]{1,0:T(8,128)(2,1)} %get-tuple-element.68.left, bf16[256,4096]{1,0:T(8,128)(2,1)} %get-tuple-element.69.right), custom_call_target="tpu_custom_call" | custom-call | flops 2147483648 | bytes 11010048 | tf_op jit(solution)/shard_map/pallas_call | solution.py:36
  69.1 8.4 %shard_map.289 = bf16[4096,1024]{1,0:T(8,128)(2,1)} custom-call(bf16[256,4096]{1,0:T(8,128)(2,1)} %get-tuple-element.70.left, bf16[256,1024]{1,0:T(8,128)(2,1)} %get-tuple-element.71.right), custom_call_target="tpu_custom_call" | custom-call | flops 2147483648 | bytes 11010048 | tf_op jit(solution)/shard_map/pallas_call | solution.py:36
  100.6 10.0 %shard_map.284 = (bf16[1024,1024]{1,0:T(8,128)(2,1)}, bf16[256,1024]{1,0:T(8,128)(2,1)}, f32[256,512]{1,0:T(8,128)}, bf16[256,512]{1,0:T(8,128)(2,1)}) custom-call(bf16[256,512]{1,0:T(8,128)(2,1)} %get-tuple-element.45.qo, bf16[256,512]{1,0:T(8,128)(2,1)} %copy-done.18, bf16[1024,512]{1,0:T(8,128)(2,1)} %get-tuple-element.47.kp, ...), custom_call_target="tpu_custom_call" | custom-call | flops 3355443200 | bytes 7340032 | tf_op jit(solution)/shard_map/pallas_call | solution.py:36
  110.7 7.0 %shard_map.287 = bf16[1024,1024]{1,0:T(8,128)(2,1)} custom-call(bf16[1024,1024]{1,0:T(8,128)(2,1)} %get-tuple-element.66.media, bf16[256,1024]{1,0:T(8,128)(2,1)} %get-tuple-element.46.latent_norm.norm.latent, bf16[1024,1024]{1,0:T(8,128)(2,1)} %get-tuple-element.58.dkvp, bf16[256,1024]{1,0:T(8,128)(2,1)} %get-tuple-element.60.dkvl), custom_call_target="tpu_custom_call" | custom-call | flops 2684354560 | bytes 7340032 | tf_op jit(solution)/shard_map/pallas_call | solution.py:36
  123.8 7.9 %shard_map.285 = (f32[1024,1024]{1,0:T(8,128)}, f32[2,1024]{1,0:T(2,128)}) custom-call(bf16[1024,1024]{1,0:T(8,128)(2,1)} %bitcast.410, bf16[1024,1024]{1,0:T(8,128)(2,1)} %get-tuple-element.58.dkvp, bf16[1024,512]{1,0:T(8,128)(2,1)} %wk.5, bf16[1024,512]{1,0:T(8,128)(2,1)} %wv.5, f32[1,1024]{1,0:T(1,128)} %bitcast.417), custom_call_target="tpu_custom_call" | custom-call | flops 2147483648 | bytes 10498048 | tf_op jit(solution)/shard_map/pallas_call | solution.py:36
  132.4 5.6 %shard_map.286 = (f32[256,1024]{1,0:T(8,128)}, bf16[1024,512]{1,0:T(8,128)(2,1)}, f32[2,1024]{1,0:T(2,128)}) custom-call(bf16[256,1024]{1,0:T(8,128)(2,1)} %bitcast.394, bf16[256,1024]{1,0:T(8,128)(2,1)} %get-tuple-element.46.latent_norm.norm.latent, bf16[256,1024]{1,0:T(8,128)(2,1)} %get-tuple-element.60.dkvl, f32[256,512]{1,0:T(8,128)} %get-tuple-element.61.dqo, ...), custom_call_target="tpu_custom_call" | custom-call | flops 1073741824 | bytes 8663040 | tf_op jit(solution)/shard_map/pallas_call | solution.py:36
  183.0 5.8 %collective-permute-done.17 = bf16[2,2,2,32,384]{4,3,2,0,1:T(8,128)(2,1)S(1)} collective-permute-done((bf16[2,2,2,32,384]{4,3,2,0,1:T(8,128)(2,1)S(1)}, bf16[2,2,2,32,384]{4,3,2,0,1:T(8,128)(2,1)S(1)}, u32[]{:S(2)}, u32[]{:S(2)}) %collective-permute-start.17) | collective-permute-done | bytes 196640 | tf_op jit(solution)/shard_map/ppermute | solution.py:333
  190.4 5.0 %collective-permute-done.12 = bf16[2,2,2,32,384]{4,3,0,1,2:T(8,128)(2,1)S(1)} collective-permute-done((bf16[2,2,2,32,384]{4,3,0,1,2:T(8,128)(2,1)S(1)}, bf16[2,2,2,32,384]{4,3,0,1,2:T(8,128)(2,1)S(1)}, u32[]{:S(2)}, u32[]{:S(2)}) %collective-permute-start.12) | collective-permute-done | bytes 196640 | tf_op jit(solution)/shard_map/ppermute | solution.py:333
  196.1 4.2 %collective-permute-done.28 = bf16[2,2,16,1024]{3,2,1,0:T(8,128)(2,1)S(1)} collective-permute-done((bf16[2,2,16,1024]{3,2,1,0:T(8,128)(2,1)S(1)}, bf16[2,2,16,1024]{3,2,1,0:T(8,128)(2,1)S(1)}, u32[]{:S(2)}, u32[]{:S(2)}) %collective-permute-start.28) | collective-permute-done | bytes 131104 | tf_op jit(solution)/shard_map/ppermute | solution.py:333
  211.6 4.0 %collective-permute-done.29 = bf16[2,16,1024]{2,1,0:T(8,128)(2,1)S(1)} collective-permute-done((bf16[2,16,1024]{2,1,0:T(8,128)(2,1)S(1)}, bf16[2,16,1024]{2,1,0:T(8,128)(2,1)S(1)}, u32[]{:S(2)}, u32[]{:S(2)}) %collective-permute-start.29) | collective-permute-done | bytes 65568 | tf_op jit(solution)/shard_map/ppermute | solution.py:333
  216.8 4.1 %collective-permute-done.19 = bf16[2,32,384]{2,1,0:T(8,128)(2,1)S(1)} collective-permute-done((bf16[2,32,384]{2,1,0:T(8,128)(2,1)S(1)}, bf16[2,32,384]{2,1,0:T(8,128)(2,1)S(1)}, u32[]{:S(2)}, u32[]{:S(2)}) %collective-permute-start.19) | collective-permute-done | bytes 49184 | tf_op jit(solution)/shard_map/ppermute | solution.py:333
  221.0 4.0 %collective-permute-done.14 = bf16[2,32,384]{2,1,0:T(8,128)(2,1)S(1)} collective-permute-done((bf16[2,32,384]{2,1,0:T(8,128)(2,1)S(1)}, bf16[2,32,384]{2,1,0:T(8,128)(2,1)S(1)}, u32[]{:S(2)}, u32[]{:S(2)}) %collective-permute-start.14) | collective-permute-done | bytes 49184 | tf_op jit(solution)/shard_map/ppermute | solution.py:333
  239.8 6.0 %collective-permute-done.7 = bf16[2,2,2,32,512]{4,3,0,1,2:T(8,128)(2,1)S(1)} collective-permute-done((bf16[2,2,2,32,512]{4,3,0,1,2:T(8,128)(2,1)S(1)}, bf16[2,2,2,32,512]{4,3,0,1,2:T(8,128)(2,1)S(1)}, u32[]{:S(2)}, u32[]{:S(2)}) %collective-permute-start.7) | collective-permute-done | bytes 262176 | tf_op jit(solution)/shard_map/ppermute | solution.py:333
  254.4 12.4 %collective-permute-done.9 = bf16[2,32,512]{2,1,0:T(8,128)(2,1)S(1)} collective-permute-done((bf16[2,32,512]{2,1,0:T(8,128)(2,1)S(1)}, bf16[2,32,512]{2,1,0:T(8,128)(2,1)S(1)}, u32[]{:S(2)}, u32[]{:S(2)}) %collective-permute-start.9) | collective-permute-done | bytes 65568 | tf_op jit(solution)/shard_map/ppermute | solution.py:333
  267.7 4.1 %collective-permute-done.10 = bf16[32,512]{1,0:T(8,128)(2,1)S(1)} collective-permute-done((bf16[32,512]{1,0:T(8,128)(2,1)S(1)}, bf16[32,512]{1,0:T(8,128)(2,1)S(1)}, u32[]{:S(2)}, u32[]{:S(2)}) %collective-permute-start.10) | collective-permute-done | bytes 32800 | tf_op jit(solution)/shard_map/ppermute | solution.py:333
  280.5 11.9 %collective-permute-done.57 = bf16[2,2,2,128,256]{4,3,1,2,0:T(8,128)(2,1)S(1)} collective-permute-done((bf16[2,2,2,128,256]{4,3,1,2,0:T(8,128)(2,1)S(1)}, bf16[2,2,2,128,256]{4,3,1,2,0:T(8,128)(2,1)S(1)}, u32[]{:S(2)}, u32[]{:S(2)}) %collective-permute-start.57) | collective-permute-done | bytes 524320 | tf_op jit(solution)/shard_map/ppermute | solution.py:333
  297.4 10.2 %collective-permute-done.58 = bf16[2,2,128,256]{3,2,0,1:T(8,128)(2,1)S(1)} collective-permute-done((bf16[2,2,128,256]{3,2,0,1:T(8,128)(2,1)S(1)}, bf16[2,2,128,256]{3,2,0,1:T(8,128)(2,1)S(1)}, u32[]{:S(2)}, u32[]{:S(2)}) %collective-permute-start.58) | collective-permute-done | bytes 262176 | tf_op jit(solution)/shard_map/ppermute | solution.py:333
  308.3 23.0 %collective-permute-done.44 = bf16[2,32,1024]{2,1,0:T(8,128)(2,1)S(1)} collective-permute-done((bf16[2,32,1024]{2,1,0:T(8,128)(2,1)S(1)}, bf16[2,32,1024]{2,1,0:T(8,128)(2,1)S(1)}, u32[]{:S(2)}, u32[]{:S(2)}) %collective-permute-start.44) | collective-permute-done | bytes 131104 | tf_op jit(solution)/shard_map/ppermute | solution.py:333
  351.4 9.1 %collective-permute-done.38 = bf16[2,2,32,1536]{3,2,1,0:T(8,128)(2,1)S(1)} collective-permute-done((bf16[2,2,32,1536]{3,2,1,0:T(8,128)(2,1)S(1)}, bf16[2,2,32,1536]{3,2,1,0:T(8,128)(2,1)S(1)}, u32[]{:S(2)}, u32[]{:S(2)}) %collective-permute-start.38) | collective-permute-done | bytes 393248 | tf_op jit(solution)/shard_map/ppermute | solution.py:333
  363.4 9.0 %collective-permute-done.53 = bf16[2,2,128,384]{3,2,1,0:T(8,128)(2,1)S(1)} collective-permute-done((bf16[2,2,128,384]{3,2,1,0:T(8,128)(2,1)S(1)}, bf16[2,2,128,384]{3,2,1,0:T(8,128)(2,1)S(1)}, u32[]{:S(2)}, u32[]{:S(2)}) %collective-permute-start.53) | collective-permute-done | bytes 393248 | tf_op jit(solution)/shard_map/ppermute | solution.py:333
  (314 shorter events, 180.4 us)
Async XLA Ops:
  81.1 19.5 %collective-permute-start.3 = (bf16[256,512]{1,0:T(8,128)(2,1)S(1)}, bf16[256,512]{1,0:T(8,128)(2,1)}, u32[]{:S(2)}, u32[]{:S(2)}) collective-permute-start(bf16[256,512]{1,0:T(8,128)(2,1)S(1)} %copy-done.20), channel_id=1, source_target_pairs={{0,1},{1,0},{2,3},{3,2},{4,5},{5,4},{6,7},{7,6},{8,9},{9,8},{10,11... | collective-permute-start | bytes 786440 | tf_op jit(solution)/shard_map/ppermute | solution.py:317
  81.5 18.0 %collective-permute-start.4 = (f32[256,128]{1,0:T(8,128)S(1)}, f32[256,128]{1,0:T(8,128)S(1)}, u32[]{:S(2)}, u32[]{:S(2)}) collective-permute-start(f32[256,128]{1,0:T(8,128)S(1)} %copy-done.23), channel_id=1, source_target_pairs={{0,1},{1,0},{2,3},{3,2},{4,5},{5,4},{6,7},{7,6},{8,9},{9,8},{10,11... | collective-permute-start | bytes 393224 | tf_op jit(solution)/shard_map/ppermute | solution.py:317
  85.0 56.8 %collective-permute-start.26 = (bf16[2,2,2,2,16,1024]{5,4,3,0,1,2:T(8,128)(2,1)}, bf16[2,2,2,2,16,1024]{5,4,3,0,1,2:T(8,128)(2,1)}, u32[]{:S(2)}, u32[]{:S(2)}) collective-permute-start(bf16[2,2,2,2,16,1024]{5,4,3,0,1,2:T(8,128)(2,1)} %bitcast.376), channel_id=1, source_target_pairs={{0,2},{2,0},{4,6},{6,4},{8,10},{10,8},{12,14},{14,12},{16,18},{18,... | collective-permute-start | bytes 1572872 | tf_op jit(solution)/shard_map/ppermute | solution.py:333
  87.2 158.7 %collective-permute-start.41 = (bf16[2,2,2,2,32,1024]{5,4,2,3,0,1:T(8,128)(2,1)}, bf16[2,2,2,2,32,1024]{5,4,2,3,0,1:T(8,128)(2,1)}, u32[]{:S(2)}, u32[]{:S(2)}) collective-permute-start(bf16[2,2,2,2,32,1024]{5,4,2,3,0,1:T(8,128)(2,1)} %bitcast.375), channel_id=1, source_target_pairs={{0,2},{2,0},{4,6},{6,4},{8,10},{10,8},{12,14},{14,12},{16,18},{18,... | collective-permute-start | bytes 3145736 | tf_op jit(solution)/shard_map/ppermute | solution.py:333
  91.2 181.7 %collective-permute-start.36 = (bf16[2,2,2,2,32,1536]{5,4,3,0,1,2:T(8,128)(2,1)}, bf16[2,2,2,2,32,1536]{5,4,3,0,1,2:T(8,128)(2,1)}, u32[]{:S(2)}, u32[]{:S(2)}) collective-permute-start(bf16[2,2,2,2,32,1536]{5,4,3,0,1,2:T(8,128)(2,1)} %bitcast.372), channel_id=1, source_target_pairs={{0,2},{2,0},{4,6},{6,4},{8,10},{10,8},{12,14},{14,12},{16,18},{18,... | collective-permute-start | bytes 4718600 | tf_op jit(solution)/shard_map/ppermute | solution.py:333
  100.1 177.1 %collective-permute-start.31 = (bf16[2,2,2,2,32,1536]{5,4,0,1,2,3:T(8,128)(2,1)}, bf16[2,2,2,2,32,1536]{5,4,0,1,2,3:T(8,128)(2,1)}, u32[]{:S(2)}, u32[]{:S(2)}) collective-permute-start(bf16[2,2,2,2,32,1536]{5,4,0,1,2,3:T(8,128)(2,1)} %bitcast.373), channel_id=1, source_target_pairs={{0,2},{2,0},{4,6},{6,4},{8,10},{10,8},{12,14},{14,12},{16,18},{18,... | collective-permute-start | bytes 4718600 | tf_op jit(solution)/shard_map/ppermute | solution.py:333
  143.3 21.7 %collective-permute-start.16 = (bf16[2,2,2,2,32,384]{5,4,3,0,1,2:T(8,128)(2,1)S(1)}, bf16[2,2,2,2,32,384]{5,4,3,0,1,2:T(8,128)(2,1)S(1)}, u32[]{:S(2)}, u32[]{:S(2)}) collective-permute-start(bf16[2,2,2,2,32,384]{5,4,3,0,1,2:T(8,128)(2,1)S(1)} %bitcast.402), channel_id=1, source_target_pairs={{0,2},{2,0},{4,6},{6,4},{8,10},{10,8},{12,14},{14,12},{16,18},{18,... | collective-permute-start | bytes 1179656 | tf_op jit(solution)/shard_map/ppermute | solution.py:333
  165.0 16.5 %collective-permute-start.27 = (bf16[2,2,2,16,1024]{4,3,2,0,1:T(8,128)(2,1)S(1)}, bf16[2,2,2,16,1024]{4,3,2,0,1:T(8,128)(2,1)S(1)}, u32[]{:S(2)}, u32[]{:S(2)}) collective-permute-start(bf16[2,2,2,16,1024]{4,3,2,0,1:T(8,128)(2,1)S(1)} %dynamic-slice_bitcast_fusion.12), channel_id=1, source_target_pairs={{0,4},{2,6},{4,0},{6,2},{8,12},{10,14},{12,8},{14,10},{16,20},{18,... | collective-permute-start | bytes 786440 | tf_op jit(solution)/shard_map/ppermute | solution.py:333
  181.4 51.3 %collective-permute-start.6 = (bf16[2,2,2,2,32,512]{5,4,0,1,2,3:T(8,128)(2,1)S(1)}, bf16[2,2,2,2,32,512]{5,4,0,1,2,3:T(8,128)(2,1)S(1)}, u32[]{:S(2)}, u32[]{:S(2)}) collective-permute-start(bf16[2,2,2,2,32,512]{5,4,0,1,2,3:T(8,128)(2,1)S(1)} %bitcast.400), channel_id=1, source_target_pairs={{0,2},{2,0},{4,6},{6,4},{8,10},{10,8},{12,14},{14,12},{16,18},{18,... | collective-permute-start | bytes 1572872 | tf_op jit(solution)/shard_map/ppermute | solution.py:333
  232.7 19.2 %collective-permute-start.56 = (bf16[2,2,2,2,128,256]{5,4,2,3,0,1:T(8,128)(2,1)S(1)}, bf16[2,2,2,2,128,256]{5,4,2,3,0,1:T(8,128)(2,1)S(1)}, u32[]{:S(2)}, u32[]{:S(2)}) collective-permute-start(bf16[2,2,2,2,128,256]{5,4,2,3,0,1:T(8,128)(2,1)S(1)} %bitcast.397), channel_id=1, source_target_pairs={{0,2},{2,0},{4,6},{6,4},{8,10},{10,8},{12,14},{14,12},{16,18},{18,... | collective-permute-start | bytes 3145736 | tf_op jit(solution)/shard_map/ppermute | solution.py:333
  245.8 48.3 %collective-permute-start.51 = (bf16[2,2,2,2,128,384]{5,4,3,0,1,2:T(8,128)(2,1)S(1)}, bf16[2,2,2,2,128,384]{5,4,3,0,1,2:T(8,128)(2,1)S(1)}, u32[]{:S(2)}, u32[]{:S(2)}) collective-permute-start(bf16[2,2,2,2,128,384]{5,4,3,0,1,2:T(8,128)(2,1)S(1)} %bitcast.396), channel_id=1, source_target_pairs={{0,2},{2,0},{4,6},{6,4},{8,10},{10,8},{12,14},{14,12},{16,18},{18,... | collective-permute-start | bytes 4718600 | tf_op jit(solution)/shard_map/ppermute | solution.py:333
  251.9 20.6 %collective-permute-start.42 = (bf16[2,2,2,32,1024]{4,3,1,2,0:T(8,128)(2,1)S(1)}, bf16[2,2,2,32,1024]{4,3,1,2,0:T(8,128)(2,1)S(1)}, u32[]{:S(2)}, u32[]{:S(2)}) collective-permute-start(bf16[2,2,2,32,1024]{4,3,1,2,0:T(8,128)(2,1)S(1)} %dynamic-slice_bitcast_fusion.5), channel_id=1, source_target_pairs={{0,8},{2,10},{4,12},{6,14},{8,0},{10,2},{12,4},{14,6},{16,24},{18,... | collective-permute-start | bytes 1572872 | tf_op jit(solution)/shard_map/ppermute | solution.py:333
  252.0 14.9 %collective-permute-start.9 = (bf16[2,32,512]{2,1,0:T(8,128)(2,1)S(1)}, bf16[2,32,512]{2,1,0:T(8,128)(2,1)S(1)}, u32[]{:S(2)}, u32[]{:S(2)}) collective-permute-start(bf16[2,32,512]{2,1,0:T(8,128)(2,1)S(1)} %dynamic-slice_bitcast_fusion.35), channel_id=1, source_target_pairs={{0,8},{2,10},{4,12},{6,14},{8,0},{10,2},{12,4},{14,6},{16,24},{18,... | collective-permute-start | bytes 196616 | tf_op jit(solution)/shard_map/ppermute | solution.py:333
  271.9 22.9 %collective-permute-start.46 = (bf16[2,2,2,2,128,384]{5,4,0,1,2,3:T(8,128)(2,1)S(1)}, bf16[2,2,2,2,128,384]{5,4,0,1,2,3:T(8,128)(2,1)S(1)}, u32[]{:S(2)}, u32[]{:S(2)}) collective-permute-start(bf16[2,2,2,2,128,384]{5,4,0,1,2,3:T(8,128)(2,1)S(1)} %bitcast.395), channel_id=1, source_target_pairs={{0,2},{2,0},{4,6},{6,4},{8,10},{10,8},{12,14},{14,12},{16,18},{18,... | collective-permute-start | bytes 4718600 | tf_op jit(solution)/shard_map/ppermute | solution.py:333
  272.5 20.0 %collective-permute-start.57 = (bf16[2,2,2,128,256]{4,3,1,2,0:T(8,128)(2,1)S(1)}, bf16[2,2,2,128,256]{4,3,1,2,0:T(8,128)(2,1)S(1)}, u32[]{:S(2)}, u32[]{:S(2)}) collective-permute-start(bf16[2,2,2,128,256]{4,3,1,2,0:T(8,128)(2,1)S(1)} %dynamic-slice_bitcast_fusion.4), channel_id=1, source_target_pairs={{0,8},{2,10},{4,12},{6,14},{8,0},{10,2},{12,4},{14,6},{16,24},{18,... | collective-permute-start | bytes 1572872 | tf_op jit(solution)/shard_map/ppermute | solution.py:333
  273.0 23.7 %collective-permute-start.43 = (bf16[2,2,32,1024]{3,2,0,1:T(8,128)(2,1)S(1)}, bf16[2,2,32,1024]{3,2,0,1:T(8,128)(2,1)S(1)}, u32[]{:S(2)}, u32[]{:S(2)}) collective-permute-start(bf16[2,2,32,1024]{3,2,0,1:T(8,128)(2,1)S(1)} %dynamic-slice_bitcast_fusion.11), channel_id=1, source_target_pairs={{0,16},{2,18},{4,20},{6,22},{8,24},{10,26},{12,28},{14,30},{16,0},... | collective-permute-start | bytes 786440 | tf_op jit(solution)/shard_map/ppermute | solution.py:333
  277.3 68.8 %collective-permute-start.37 = (bf16[2,2,2,32,1536]{4,3,2,0,1:T(8,128)(2,1)S(1)}, bf16[2,2,2,32,1536]{4,3,2,0,1:T(8,128)(2,1)S(1)}, u32[]{:S(2)}, u32[]{:S(2)}) collective-permute-start(bf16[2,2,2,32,1536]{4,3,2,0,1:T(8,128)(2,1)S(1)} %dynamic-slice_bitcast_fusion.2), channel_id=1, source_target_pairs={{0,4},{2,6},{4,0},{6,2},{8,12},{10,14},{12,8},{14,10},{16,20},{18,... | collective-permute-start | bytes 2359304 | tf_op jit(solution)/shard_map/ppermute | solution.py:333
  292.5 53.9 %collective-permute-start.32 = (bf16[2,2,2,32,1536]{4,3,0,1,2:T(8,128)(2,1)S(1)}, bf16[2,2,2,32,1536]{4,3,0,1,2:T(8,128)(2,1)S(1)}, u32[]{:S(2)}, u32[]{:S(2)}) collective-permute-start(bf16[2,2,2,32,1536]{4,3,0,1,2:T(8,128)(2,1)S(1)} %dynamic-slice_bitcast_fusion.3), channel_id=1, source_target_pairs={{0,1},{1,0},{2,3},{3,2},{4,5},{5,4},{6,7},{7,6},{8,9},{9,8},{10,11... | collective-permute-start | bytes 2359304 | tf_op jit(solution)/shard_map/ppermute | solution.py:333
  294.8 53.2 %collective-permute-start.52 = (bf16[2,2,2,128,384]{4,3,2,0,1:T(8,128)(2,1)S(1)}, bf16[2,2,2,128,384]{4,3,2,0,1:T(8,128)(2,1)S(1)}, u32[]{:S(2)}, u32[]{:S(2)}) collective-permute-start(bf16[2,2,2,128,384]{4,3,2,0,1:T(8,128)(2,1)S(1)} %dynamic-slice_bitcast_fusion), channel_id=1, source_target_pairs={{0,4},{2,6},{4,0},{6,2},{8,12},{10,14},{12,8},{14,10},{16,20},{18,... | collective-permute-start | bytes 2359304 | tf_op jit(solution)/shard_map/ppermute | solution.py:333
  296.7 53.6 %collective-permute-start.47 = (bf16[2,2,2,128,384]{4,3,0,1,2:T(8,128)(2,1)S(1)}, bf16[2,2,2,128,384]{4,3,0,1,2:T(8,128)(2,1)S(1)}, u32[]{:S(2)}, u32[]{:S(2)}) collective-permute-start(bf16[2,2,2,128,384]{4,3,0,1,2:T(8,128)(2,1)S(1)} %dynamic-slice_bitcast_fusion.1), channel_id=1, source_target_pairs={{0,1},{1,0},{2,3},{3,2},{4,5},{5,4},{6,7},{7,6},{8,9},{9,8},{10,11... | collective-permute-start | bytes 2359304 | tf_op jit(solution)/shard_map/ppermute | solution.py:333
  307.6 23.6 %collective-permute-start.44 = (bf16[2,32,1024]{2,1,0:T(8,128)(2,1)S(1)}, bf16[2,32,1024]{2,1,0:T(8,128)(2,1)S(1)}, u32[]{:S(2)}, u32[]{:S(2)}) collective-permute-start(bf16[2,32,1024]{2,1,0:T(8,128)(2,1)S(1)} %dynamic-slice_bitcast_fusion.21), channel_id=1, source_target_pairs={{0,1},{1,0},{2,3},{3,2},{4,5},{5,4},{6,7},{7,6},{8,9},{9,8},{10,11... | collective-permute-start | bytes 393224 | tf_op jit(solution)/shard_map/ppermute | solution.py:333
  348.3 24.1 %collective-permute-start.53 = (bf16[2,2,128,384]{3,2,1,0:T(8,128)(2,1)S(1)}, bf16[2,2,128,384]{3,2,1,0:T(8,128)(2,1)S(1)}, u32[]{:S(2)}, u32[]{:S(2)}) collective-permute-start(bf16[2,2,128,384]{3,2,1,0:T(8,128)(2,1)S(1)} %dynamic-slice_bitcast_fusion.6), channel_id=1, source_target_pairs={{0,8},{2,10},{4,12},{6,14},{8,0},{10,2},{12,4},{14,6},{16,24},{18,... | collective-permute-start | bytes 1179656 | tf_op jit(solution)/shard_map/ppermute | solution.py:333
  350.6 22.0 %collective-permute-start.48 = (bf16[2,2,128,384]{3,2,0,1:T(8,128)(2,1)S(1)}, bf16[2,2,128,384]{3,2,0,1:T(8,128)(2,1)S(1)}, u32[]{:S(2)}, u32[]{:S(2)}) collective-permute-start(bf16[2,2,128,384]{3,2,0,1:T(8,128)(2,1)S(1)} %dynamic-slice_bitcast_fusion.7), channel_id=1, source_target_pairs={{0,4},{2,6},{4,0},{6,2},{8,12},{10,14},{12,8},{14,10},{16,20},{18,... | collective-permute-start | bytes 1179656 | tf_op jit(solution)/shard_map/ppermute | solution.py:333
  360.9 16.0 %collective-permute-start.34 = (bf16[2,32,1536]{2,1,0:T(8,128)(2,1)S(1)}, bf16[2,32,1536]{2,1,0:T(8,128)(2,1)S(1)}, u32[]{:S(2)}, u32[]{:S(2)}) collective-permute-start(bf16[2,32,1536]{2,1,0:T(8,128)(2,1)S(1)} %dynamic-slice_bitcast_fusion.17), channel_id=1, source_target_pairs={{0,8},{2,10},{4,12},{6,14},{8,0},{10,2},{12,4},{14,6},{16,24},{18,... | collective-permute-start | bytes 589832 | tf_op jit(solution)/shard_map/ppermute | solution.py:333
  (70 other events, 506.1 us)

commit v2 on v1

--- a/solution.py
+++ b/solution.py
@@ -304,13 +304,352 @@
     latent, norm, dkvl, dqo, drecv, residual_grad, wq, wk, wv, gain, out, query_grad, vectors
 ):
     dq = (dqo[...] + drecv[...].astype(F32)).astype(BF)
-    query_grad[...] = (HEAD_DIM**-0.5 * t_dot(norm[...], dq)).astype(BF)
+    product = (HEAD_DIM**-0.5 * t_dot(norm[...], dq)).astype(BF)
+    if query_grad.shape == product.shape:
+        query_grad[...] = product
+    else:
+        product = product.reshape(-1, 32, INNER)
+        shape = query_grad.shape[:-1] + (INNER,)
+        query_grad[..., :INNER] = product[:, :16].reshape(shape)
+        query_grad[..., INNER:] = product[:, 16:].reshape(shape)
     grad = dot_t(dkvl[:, :INNER], wk[...]) + dot_t(dkvl[:, INNER:], wv[...])
     grad += HEAD_DIM**-0.5 * dot_t(dq, wq[...])
     unit, scale = centred(latent[...].astype(F32))
     vectors[0:1, :] = column_sum(grad * unit)
     vectors[1:2, :] = column_sum(grad)
     out[...] = residual_grad[...] + norm_back(unit, scale, gain[...], grad)
+
+
+def first_body(ints, latent, cot, gain, bias, wq, norm, query, og):
+    unit, _ = centred(latent[...].astype(F32))
+    low = (unit * gain[...] + bias[...]).astype(BF)
+    norm[...] = low
+    query[...] = (HEAD_DIM**-0.5 * dot(low, wq[...])).astype(BF)
+    count = latent.shape[0]
+    slot = lax.broadcasted_iota(jnp.int32, (count, 1), 0) // ints[6]
+    live = jnp.where(slot < ints[0], 1.0, 0.0).astype(F32)
+    og[...] = (cot[...].astype(F32) * live).astype(BF)
+
+
+def ffn_body(
+    ints,
+    oo,
+    orecv,
+    so,
+    srecv,
+    latent,
+    og,
+    wo,
+    wup,
+    wdown,
+    gain,
+    bias,
+    new_latents,
+    act_own,
+    act_send,
+    pre_out,
+    ffn_own,
+    ffn_send,
+    residual,
+    gacc,
+    attended,
+    packed,
+    ffn_in,
+    acc,
+):
+    step = pl.program_id(0)
+    count = latent.shape[0]
+    core = ints[1]
+
+    @pl.when(step == 0)
+    def _():
+        a, b = so[...], srecv[...]
+        top = jnp.maximum(a, b)
+        both = top + jnp.log(jnp.exp(a - top) + jnp.exp(b - top))
+        packed[...] = both
+        mix = widen(jnp.exp(a - both)) * oo[...]
+        mix += widen(jnp.exp(b - both)) * orecv[...].astype(F32)
+        attended[...] = mix
+        res = latent[...].astype(F32) + dot(mix.astype(BF), wo[...])
+        residual[...] = res
+        unit, _ = centred(res)
+        low = (unit * gain[...] + bias[...]).astype(BF)
+        ffn_in[...] = low
+        turned = low.T.reshape(8, 2, -1, count)
+        even, odd = turned[:, 0], turned[:, 1]
+        ffn_own[...] = jnp.where(core == 0, even, odd).reshape(ffn_own.shape)
+        ffn_send[...] = jnp.where(core == 0, odd, even).reshape(ffn_send.shape)
+        acc[...] = jnp.zeros_like(acc)
+        gacc[...] = jnp.zeros_like(gacc)
+
+    pre = dot(ffn_in[...], wup[...])
+    cdf = 0.5 * (1.0 + lax.erf(pre * (0.5**0.5)))
+    act = (pre * cdf).astype(BF)
+    turned = act.T
+    half = turned.shape[0] // 2
+    even, odd = turned[:half], turned[half:]
+    act_own[...] = jnp.where(core == 0, even, odd).reshape(act_own.shape)
+    act_send[...] = jnp.where(core == 0, odd, even).reshape(act_send.shape)
+    acc[...] += dot(act, wdown[...])
+    act_grad = dot_t(og[...], wdown[...])
+    pdf = jnp.exp(-0.5 * pre * pre) * 0.3989422804014327
+    pre_grad = (act_grad * (cdf + pre * pdf)).astype(BF)
+    pre_out[...] = pre_grad
+    gacc[...] += dot_t(pre_grad, wup[...])
+
+    @pl.when(step == pl.num_programs(0) - 1)
+    def _():
+        slot = lax.broadcasted_iota(jnp.int32, (count, 1), 0) // ints[6]
+        live = jnp.where(slot < ints[0], 1.0, 0.0).astype(F32)
+        new_latents[...] = ((residual[...] + acc[...]) * live).astype(BF)
+
+
+def ffn_back_body(
+    residual, gacc, og, mix_ref, packed, wo, gain, residual_grad, attended_grad, stats, out, vectors
+):
+    unit, scale = centred(residual[...])
+    grad = gacc[...]
+    vectors[0:1, :] = column_sum(grad * unit)
+    vectors[1:2, :] = column_sum(grad)
+    res_grad = og[...].astype(F32) + norm_back(unit, scale, gain[...], grad)
+    residual_grad[...] = res_grad
+    branch = res_grad.astype(BF)
+    back = dot_t(branch, wo[...]).astype(BF)
+    attended_grad[...] = back
+    mix = mix_ref[...]
+    product = back.astype(F32) * mix
+    head = head_of(product.shape)
+    sums = [
+        jnp.sum(jnp.where(head == h, product, 0.0), axis=-1, keepdims=True) for h in range(HEADS)
+    ]
+    delta = pack_lanes(sums)
+    lane = lax.broadcasted_iota(jnp.int32, delta.shape, 1)
+    stats[...] = jnp.where(lane % PER < PER // 2, packed[...], delta)
+    out[...] = t_dot(mix.astype(BF), branch).astype(BF).reshape(out.shape)
+
+
+def pick(ref, part, bit):
+    if part == 0:
+        v = ref[:, :, :, bit]
+    elif part == 1:
+        v = ref[:, :, bit]
+    else:
+        v = ref[:, bit]
+    return v.reshape(-1, v.shape[-1])
+
+
+def down_part_body(ints, own, sib, og, og_sib, a_out, a_keep, b_out, b_keep, c_out, c_keep):
+    step = pl.program_id(0)
+
+    def fill(part, out, keep):
+        bit = ints[2 + part]
+        for ref, b in ((out, 1 - bit), (keep, bit)):
+            v = dot(pick(own, part, b), og[...]) + dot(pick(sib, part, b), og_sib[...])
+            v = v.astype(BF).reshape(8, 4, 32, v.shape[-1])
+            wide = v.shape[-1]
+            for k in range(4):
+                ref[:, 0, :, k * wide : (k + 1) * wide] = v[:, k]
+
+    @pl.when(step < 2)
+    def _():
+        fill(0, a_out, a_keep)
+
+    @pl.when(step == 2)
+    def _():
+        fill(1, b_out, b_keep)
+
+    @pl.when(step == 3)
+    def _():
+        fill(2, c_out, c_keep)
+
+
+def up_part_body(ints, own, sib, pre, pre_sib, a_out, a_keep, b_out, b_keep, c_out, c_keep):
+    step = pl.program_id(0)
+
+    def fill(part, out, keep):
+        bit = ints[2 + part]
+        for ref, b in ((out, 1 - bit), (keep, bit)):
+            v = dot(pick(own, part, b), pre[...]) + dot(pick(sib, part, b), pre_sib[...])
+            ref[...] = v.astype(BF).reshape(ref.shape)
+
+    @pl.when(step == 0)
+    def _():
+        fill(0, a_out, a_keep)
+
+    @pl.when((step == 1) | (step == 2))
+    def _():
+        fill(1, b_out, b_keep)
+
+    @pl.when(step == 3)
+    def _():
+        fill(2, c_out, c_keep)
+
+
+def plus(a, b):
+    return a.astype(F32) + b.astype(F32)
+
+
+def reduce_body(
+    akd, ard, aku, aru, bkd, brd, bku, bru, ckd, crd, cku, cru,
+    kv, og, qg, media_vec, latent_vec, ffn_vec,
+    fin, vec,
+    wa, wb, wc, ra1, ra2, ra3, a2, a3, rb1, rb2, rb3, b2, b3, rc1, rc2, rc3, c2, c3,
+    kk, rk0, wk, rk1, k2, rk2, k3, rk3, k4, rk4,
+    kq, rq0, wq, rq1, q2, rq2, q3, rq3, q4, rq4,
+    vs, vr, load_sem, send_sem, recv_sem,
+):
+    mine = lax.axis_index("img")
+    xb = lax.axis_index("lat")
+    cb, yb, z1, z2 = mine % 2, (mine // 2) % 2, (mine // 4) % 2, (mine // 8) % 2
+
+    def to(bit, weight):
+        return (mine + weight - 2 * weight * bit, xb)
+
+    peer = {"c": to(cb, 1), "y": to(yb, 2), "z": to(z1, 4), "w": to(z2, 8), "x": (mine, 1 - xb)}
+    barrier = pltpu.get_barrier_semaphore()
+    for axis in peer:
+        pl.semaphore_signal(
+            barrier, inc=1, device_id=peer[axis], device_id_type=pl.DeviceIdType.MESH
+        )
+
+    used = []
+
+    def send(src, dst, axis):
+        slot = len(used)
+        copy = pltpu.make_async_remote_copy(
+            src_ref=src,
+            dst_ref=dst,
+            send_sem=send_sem.at[slot],
+            recv_sem=recv_sem.at[slot],
+            device_id=peer[axis],
+            device_id_type=pl.DeviceIdType.MESH,
+        )
+        copy.start()
+        used.append(copy)
+        return copy
+
+    loads = []
+    for i, (src, dst) in enumerate(
+        (
+            (kv.at[:, :, :, cb], kk),
+            (og.at[:, :, :, cb], kq.at[:, :, :, :, pl.ds(0, 16)]),
+            (qg.at[:, :, :, cb], kq.at[:, :, :, :, pl.ds(16, 16)]),
+        )
+    ):
+        loads.append(pltpu.make_async_copy(src, dst, load_sem.at[i]))
+        loads[-1].start()
+    vs[0] = jnp.zeros(vs.shape[1:], F32)
+    vs[0, 0:2, :] = media_vec[...]
+    vs[0, 2:4, :] = latent_vec[...]
+    vs[0, 4:6, :] = ffn_vec[...]
+
+    pl.semaphore_wait(barrier, len(peer))
+    q0 = send(qg.at[:, :, :, 1 - cb], rq0.at[:, :, :, :, pl.ds(16, 16)], "c")
+    o0 = send(og.at[:, :, :, 1 - cb], rq0.at[:, :, :, :, pl.ds(0, 16)], "c")
+    k0 = send(kv.at[:, :, :, 1 - cb], rk0, "c")
+    vec_order = "cxyzw"
+    vc = send(vs.at[0], vr.at[0], vec_order[0])
+
+    def vec_step(i, vc):
+        vc.wait_recv()
+        if i < 4:
+            vs[i + 1] = vs[i] + vr[i]
+            return send(vs.at[i + 1], vr.at[i + 1], vec_order[i + 1])
+        vec[...] = vs[i] + vr[i]
+
+    wa[:, :, :, 0:2] = plus(akd[...], ard[...]).astype(BF)
+    wa[:, :, :, 2:3] = plus(aku[...], aru[...]).astype(BF)
+    sa1 = send(wa.at[:, :, 1 - yb], ra1, "y")
+    wb[:, :, :, 0:1] = plus(bkd[...], brd[...]).astype(BF)
+    wb[:, :, :, 1:3] = plus(bku[...], bru[...]).astype(BF)
+    sb1 = send(wb.at[:, :, 1 - xb], rb1, "x")
+    loads[0].wait()
+    k0.wait_recv()
+    wk[...] = plus(kk[...], rk0[...]).astype(BF)
+    sk1 = send(wk.at[:, :, :, 1 - xb], rk1, "x")
+    wc[:, :, :, 0:1] = plus(ckd[...], crd[...]).astype(BF)
+    wc[:, :, :, 1:2] = plus(cku[...], cru[...]).astype(BF)
+    sc1 = send(wc.at[:, :, 1 - xb], rc1, "x")
+    loads[1].wait()
+    loads[2].wait()
+    q0.wait_recv()
+    o0.wait_recv()
+    wq[...] = plus(kq[...], rq0[...]).astype(BF)
+    sq1 = send(wq.at[:, 1 - z1], rq1, "z")
+    vc = vec_step(0, vc)
+
+    sa1.wait_recv()
+    a2[...] = plus(wa[:, :, yb], ra1[...]).astype(BF)
+    sa2 = send(a2.at[:, 1 - z1], ra2, "z")
+    sb1.wait_recv()
+    b2[...] = plus(wb[:, :, xb], rb1[...]).astype(BF)
+    sb2 = send(b2.at[:, 1 - z1], rb2, "z")
+    vc = vec_step(1, vc)
+    sk1.wait_recv()
+    k2[...] = plus(wk[:, :, :, xb], rk1[...]).astype(BF)
+    sk2 = send(k2.at[:, :, 1 - yb], rk2, "y")
+    sc1.wait_recv()
+    c2[...] = plus(wc[:, :, xb], rc1[...]).astype(BF)
+    sc2 = send(c2.at[:, 1 - yb], rc2, "y")
+    sq1.wait_recv()
+    q2[...] = plus(wq[:, z1], rq1[...]).astype(BF)
+    sq2 = send(q2.at[:, :, 1 - xb], rq2, "x")
+    vc = vec_step(2, vc)
+
+    sa2.wait_recv()
+    a3[...] = plus(a2[:, z1], ra2[...]).astype(BF)
+    sa3 = send(a3.at[1 - z2], ra3, "w")
+    sb2.wait_recv()
+    b3[...] = plus(b2[:, z1], rb2[...]).astype(BF)
+    sb3 = send(b3.at[1 - z2], rb3, "w")
+    sk2.wait_recv()
+    k3[...] = plus(k2[:, :, yb], rk2[...]).astype(BF)
+    sk3 = send(k3.at[:, 1 - z1], rk3, "z")
+    sc2.wait_recv()
+    c3[...] = plus(c2[:, yb], rc2[...]).astype(BF)
+    sc3 = send(c3.at[1 - z2], rc3, "w")
+    sq2.wait_recv()
+    q3[...] = plus(q2[:, :, xb], rq2[...]).astype(BF)
+    sq3 = send(q3.at[:, 1 - yb], rq3, "y")
+    vc = vec_step(3, vc)
+
+    sk3.wait_recv()
+    k4[...] = plus(k3[:, z1], rk3[...]).astype(BF)
+    sk4 = send(k4.at[1 - z2], rk4, "w")
+    sq3.wait_recv()
+    q4[...] = plus(q3[:, yb], rq3[...]).astype(BF)
+    sq4 = send(q4.at[1 - z2], rq4, "w")
+    sa3.wait_recv()
+    fin[0:3] = plus(a3[z2], ra3[...])
+    sb3.wait_recv()
+    fin[3:6] = plus(b3[z2], rb3[...])
+    sc3.wait_recv()
+    fin[6:8] = plus(c3[z2], rc3[...])
+    vec_step(4, vc)
+    sk4.wait_recv()
+    fin[8] = plus(k4[z2], rk4[...])
+    sq4.wait_recv()
+    fin[9] = plus(q4[z2], rq4[...])
+    for copy in used:
+        copy.wait_send()
+
+
+def unpack_body(ints, fin, vec, up, down, key, value, out, query, thin):
+    for g, i in enumerate((2, 4, 5, 7)):
+        up[:, g * 1024 : (g + 1) * 1024] = fin[i]
+    for g, i in enumerate((0, 1, 3, 6)):
+        for k in range(4):
+            down[k * 32 : (k + 1) * 32, g * 256 : (g + 1) * 256] = fin[
+                i, :, k * 256 : (k + 1) * 256
+            ]
+    key[...] = fin[8, :, :INNER]
+    value[...] = fin[8, :, INNER:]
+    out[...] = fin[9, 0:16]
+    query[0:16] = fin[9, 16:32, :INNER]
+    query[16:32] = fin[9, 16:32, INNER:]
+    width = vec.shape[1]
+    turned = pltpu.roll(vec[...], width - ints[5] * 32, 1)
+    thin[...] = turned[:, :LANES]
 
 
 def swap_lat(v):
@@ -609,12 +948,381 @@
     )
 
 
+def fits(mesh):
+    return mesh.shape["img"] == 16 and mesh.shape["lat"] == 2
+
+
+def quick(
+    count,
+    patches,
+    latents,
+    cotangent,
+    doc_images,
+    doc_device,
+    query_weight,
+    key_weight,
+    value_weight,
+    output_weight,
+    up_weight,
+    down_weight,
+    media_gain,
+    media_bias,
+    latent_gain,
+    latent_bias,
+    ffn_gain,
+    ffn_bias,
+):
+    slots, own_patches, width = patches.shape
+    own_latents = latents.shape[1]
+    hidden = up_weight.shape[1]
+    np_, nl = slots * own_patches, slots * own_latents
+    mine, lat = lax.axis_index("img"), lax.axis_index("lat")
+    holding = jnp.sum(jnp.where(doc_device == mine, doc_images, 0))
+    ints = jnp.stack(
+        [
+            holding,
+            mine % 2,
+            lat,
+            (mine // 2) % 2,
+            (mine // 4) % 2,
+            mine * 2 + lat,
+            jnp.int32(own_latents),
+            jnp.int32(0),
+        ]
+    ).astype(jnp.int32)
+    sspec = pl.BlockSpec(memory_space=pltpu.SMEM)
+    patch = patches.reshape(np_, width)
+    latent = latents.reshape(nl, width)
+    cot = cotangent.reshape(nl, width)
+    mg, mb = media_gain.reshape(1, width), media_bias.reshape(1, width)
+    lg, lb = latent_gain.reshape(1, width), latent_bias.reshape(1, width)
+    fg, fb = ffn_gain.reshape(1, width), ffn_bias.reshape(1, width)
+    wspec = whole((width, INNER))
+    vspec = whole((1, width))
+    lspec = whole((nl, width))
+    nspec = whole((nl, INNER))
+    core_pairs = [(i, i ^ 1) for i in range(count)]
+
+    def sibling(v):
+        return lax.ppermute(v, "img", core_pairs)
+
+    norm_l, query, out_grad = call(
+        first_body,
+        (1,),
+        [sspec, lspec, lspec, vspec, vspec, wspec],
+        [
+            (struct((nl, width), BF), lspec),
+            (struct((nl, INNER), BF), nspec),
+            (struct((nl, width), BF), lspec),
+        ],
+        (ints, latent, cot, lg, lb, query_weight),
+        2 * nl * width * INNER,
+    )
+    query_peer = swap_lat(query)
+    og_sib = sibling(out_grad)
+    blk = 256
+    norm_m, kp, vp, kl, vl = call(
+        media_body,
+        (np_ // blk,),
+        [rows(blk, width), vspec, vspec, wspec, wspec, lspec],
+        [
+            (struct((np_, width), BF), rows(blk, width)),
+            (struct((np_, INNER), BF), rows(blk, INNER)),
+            (struct((np_, INNER), BF), rows(blk, INNER)),
+            (struct((nl, INNER), BF), nspec),
+            (struct((nl, INNER), BF), nspec),
+        ],
+        (patch, mg, mb, key_weight, value_weight, norm_l),
+        4 * (np_ + nl) * width * INNER,
+    )
+    q_s, p_s, s_s = rows(own_latents, INNER), rows(own_patches, INNER), rows(own_latents, LANES)
+    att_flops = 4 * slots * (own_patches + own_latents) * INNER * INNER
+    o_own, o_peer, s_own, s_peer = call(
+        attend_body,
+        (slots,),
+        [q_s, q_s, p_s, p_s, q_s, q_s],
+        [
+            (struct((nl, INNER), F32), q_s),
+            (struct((nl, INNER), BF), q_s),
+            (struct((nl, LANES), F32), s_s),
+            (struct((nl, LANES), F32), s_s),
+        ],
+        (query, query_peer, kp, vp, kl, vl),
+        att_flops,
+    )
+    o_recv, s_recv = swap_lat(o_peer), swap_lat(s_peer)
+    fblk = hidden // 8
+    turned = (2, 2, 2, 2, fblk // 4, nl)
+    turned_spec = pl.BlockSpec(
+        (1, 1, 1) + turned[3:], lambda i: (i // 4, (i // 2) % 2, i % 2, 0, 0, 0)
+    )
+    ffn_turned = (2, 2, 2, 2, width // (2 * count), nl)
+    stat = whole((nl, LANES))
+    (
+        new_latents,
+        act_own,
+        act_send,
+        pre_grad,
+        ffn_own,
+        ffn_send,
+        residual,
+        gacc,
+        attended,
+        packed,
+    ) = call(
+        ffn_body,
+        (8,),
+        [
+            sspec,
+            nspec,
+            nspec,
+            stat,
+            stat,
+            lspec,
+            lspec,
+            whole((INNER, width)),
+            cols(width, fblk),
+            rows(fblk, width),
+            vspec,
+            vspec,
+        ],
+        [
+            (struct((nl, width), BF), lspec),
+            (struct(turned, BF), turned_spec),
+            (struct(turned, BF), turned_spec),
+            (struct((nl, hidden), BF), cols(nl, fblk)),
+            (struct(ffn_turned, BF), whole(ffn_turned)),
+            (struct(ffn_turned, BF), whole(ffn_turned)),
+            (struct((nl, width), F32), lspec),
+            (struct((nl, width), F32), lspec),
+            (struct((nl, INNER), F32), nspec),
+            (struct((nl, LANES), F32), stat),
+        ],
+        (
+            ints,
+            o_own,
+            o_recv,
+            s_own,
+            s_recv,
+            latent,
+            out_grad,
+            output_weight,
+            up_weight,
+            down_weight,
+            fg,
+            fb,
+        ),
+        8 * nl * width * hidden,
+        scratch=[pltpu.VMEM((nl, width), BF), pltpu.VMEM((nl, width), F32)],
+    )
+    act_sib, pre_sib, ffn_sib = sibling(act_send), sibling(pre_grad), sibling(ffn_send)
+    o_shape = (2, 2, 2, 2, 2, INNER // (2 * count), width)
+    residual_grad, attended_grad, stats, output_grad, ffn_vec = call(
+        ffn_back_body,
+        (1,),
+        [lspec, lspec, lspec, nspec, stat, whole((INNER, width)), vspec],
+        [
+            (struct((nl, width), F32), lspec),
+            (struct((nl, INNER), BF), nspec),
+            (struct((nl, LANES), F32), stat),
+            (struct(o_shape, BF), whole(o_shape)),
+            (struct((2, width), F32), whole((2, width))),
+        ],
+        (residual, gacc, out_grad, attended, packed, output_weight, fg),
+        4 * nl * width * INNER,
+    )
+    grad_peer, stats_peer = swap_lat(attended_grad), swap_lat(stats)
+
+    def part_outs(counts, first):
+        outs = []
+        for n, start in zip(counts, first):
+            shape = (8, n, 32, 1024)
+            spec = pl.BlockSpec(
+                (8, 1, 32, 1024),
+                lambda i, n=n, start=start: (0, jnp.clip(i - start, 0, n - 1), 0, 0),
+            )
+            outs += [(struct(shape, BF), spec)] * 2
+        return outs
+
+    def hops(parts):
+        pairs = [[(i, i ^ 2) for i in range(count)], [(i, i ^ 4) for i in range(count)]]
+        return (
+            swap_lat(parts[0]),
+            parts[1],
+            lax.ppermute(parts[2], "img", pairs[0]),
+            parts[3],
+            lax.ppermute(parts[4], "img", pairs[1]),
+            parts[5],
+        )
+
+    down_parts = call(
+        down_part_body,
+        (4,),
+        [sspec, whole(turned), whole(turned), cols(nl, width // 4), cols(nl, width // 4)],
+        part_outs((2, 1, 1), (0, 2, 3)),
+        (ints, act_own, act_sib, out_grad, og_sib),
+        2 * nl * width * hidden,
+    )
+    ard, akd, brd, bkd, crd, ckd = hops(down_parts)
+    up_parts = call(
+        up_part_body,
+        (4,),
+        [sspec, whole(ffn_turned), whole(ffn_turned), cols(nl, hidden // 4), cols(nl, hidden // 4)],
+        part_outs((1, 2, 1), (0, 1, 3)),
+        (ints, ffn_own, ffn_sib, pre_grad, pre_sib),
+        2 * nl * width * hidden,
+    )
+    aru, aku, bru, bku, cru, cku = hops(up_parts)
+    dkvp, dkvl, dq_own, dq_peer = call(
+        attend_back_body,
+        (slots,),
+        [q_s, q_s, p_s, p_s, q_s, q_s, q_s, q_s, s_s, s_s],
+        [
+            (struct((np_, 2 * INNER), BF), rows(own_patches, 2 * INNER)),
+            (struct((nl, 2 * INNER), BF), rows(own_latents, 2 * INNER)),
+            (struct((nl, INNER), F32), q_s),
+            (struct((nl, INNER), BF), q_s),
+        ],
+        (query, query_peer, kp, vp, kl, vl, attended_grad, grad_peer, stats, stats_peer),
+        att_flops * 5 // 2,
+    )
+    dq_recv = swap_lat(dq_peer)
+    kblk = 256
+    (kv_grad,) = call(
+        kv_grad_body,
+        (2 * INNER // kblk,),
+        [whole((np_, width)), lspec, cols(np_, kblk), cols(nl, kblk)],
+        [(struct((width, 2 * INNER), BF), cols(width, kblk))],
+        (norm_m, norm_l, dkvp, dkvl),
+        4 * (np_ + nl) * width * INNER,
+    )
+    patches_grad, media_vec = call(
+        patch_back_body,
+        (np_ // blk,),
+        [rows(blk, width), rows(blk, 2 * INNER), wspec, wspec, vspec],
+        [(struct((np_, width), F32), rows(blk, width)), (struct((2, width), F32), whole((2, width)))],
+        (patch, dkvp, key_weight, value_weight, mg),
+        4 * np_ * width * INNER,
+    )
+    latents_grad, query_grad, latent_vec = call(
+        latent_back_body,
+        (1,),
+        [
+            lspec,
+            lspec,
+            whole((nl, 2 * INNER)),
+            nspec,
+            nspec,
+            lspec,
+            wspec,
+            wspec,
+            wspec,
+            vspec,
+        ],
+        [
+            (struct((nl, width), F32), lspec),
+            (struct(o_shape, BF), whole(o_shape)),
+            (struct((2, width), F32), whole((2, width))),
+        ],
+        (
+            latent,
+            norm_l,
+            dkvl,
+            dq_own,
+            dq_recv,
+            residual_grad,
+            query_weight,
+            key_weight,
+            value_weight,
+            lg,
+        ),
+        8 * nl * width * INNER,
+    )
+    block = (32, 1024)
+    eight = [
+        v.reshape((2, 2, 2, v.shape[1]) + block)
+        for v in (akd, ard, aku, aru, bkd, brd, bku, bru, ckd, crd, cku, cru)
+    ]
+    kv = kv_grad.reshape((2, 2, 2, 2, 2) + block)
+    inputs = eight + [kv, output_grad, query_grad, media_vec, latent_vec, ffn_vec]
+    vmem = pl.BlockSpec(memory_space=pltpu.VMEM)
+    hbm = pl.BlockSpec(memory_space=pl.ANY)
+
+    def ladder(n):
+        mid = (n,) + block
+        return [(2, 2) + mid, (2,) + mid, mid], [(2, 2) + mid, (2,) + mid]
+
+    scratch = [(2, 2, 2, n) + block for n in (3, 3, 2)]
+    for n in (3, 3, 2):
+        got, sums = ladder(n)
+        scratch += got + sums
+    for _ in range(2):
+        full = (2, 2, 2, 2) + block
+        scratch += [full, full, full]
+        for k in (3, 2, 1):
+            scratch += [(2,) * k + block] * 2
+        scratch += [block]
+    scratch = [pltpu.VMEM(shape, BF) for shape in scratch]
+    copies = 24
+    fin, vec = pl.pallas_call(
+        reduce_body,
+        in_specs=[vmem] * 12 + [hbm] * 3 + [vmem] * 3,
+        out_specs=[vmem, vmem],
+        out_shape=[struct((10,) + block, F32), struct((8, width), F32)],
+        scratch_shapes=scratch
+        + [
+            pltpu.VMEM((5, 8, width), F32),
+            pltpu.VMEM((5, 8, width), F32),
+            pltpu.SemaphoreType.DMA((3,)),
+            pltpu.SemaphoreType.DMA((copies + 1,)),
+            pltpu.SemaphoreType.DMA((copies + 1,)),
+        ],
+        compiler_params=pltpu.CompilerParams(
+            collective_id=0, has_side_effects=True, vmem_limit_bytes=VMEM_LIMIT
+        ),
+    )(*inputs)
+    d = 2 * count
+    shapes = [
+        (width // d, hidden),
+        (hidden // d, width),
+        (width // d, INNER),
+        (width // d, INNER),
+        (INNER // d, width),
+        (width // d, INNER),
+        (8, LANES),
+    ]
+    up_sum, down_sum, key_sum, value_sum, output_sum, query_sum, thin = pl.pallas_call(
+        unpack_body,
+        in_specs=[sspec, vmem, vmem],
+        out_specs=[vmem] * 7,
+        out_shape=[struct(shape, F32) for shape in shapes],
+    )(ints, fin, vec)
+    thin = thin[:, : width // d]
+    return (
+        new_latents.reshape(latents.shape),
+        patches_grad.reshape(patches.shape),
+        latents_grad.reshape(latents.shape),
+        query_sum,
+        key_sum,
+        value_sum,
+        output_sum,
+        up_sum,
+        down_sum,
+        thin[0],
+        thin[1],
+        thin[2],
+        thin[3],
+        thin[4],
+        thin[5],
+    )
+
+
 def solution(mesh):
     split = P("img", "lat", None)
     both = P(("img", "lat"), None)
     line = P(("img", "lat"))
     return jax.shard_map(
-        partial(local, mesh.shape["img"]),
+        partial(quick if fits(mesh) else local, mesh.shape["img"]),
         mesh=mesh,
         in_specs=(split,) * 3 + (P(),) * 14,
         out_specs=(split,) * 3 + (both,) * 6 + (line,) * 6,

time: 391 us -> 219 us (0.56)
  waiting for transfers between devices: 175 us -> 13.7 us
  Pallas kernels: 88.8 us -> 176 us
  starting transfers between devices: 70.6 us -> 16.1 us
  local copies, waits for them, and re-layouts: 35.5 us -> 9.56 us
  other arithmetic: 17.7 us -> 1.31 us
    ppermute x60 -> x8, waiting for transfers between devices: 167 us -> 0.02 us  [the longest x4 0.01 us: sibling(): return lax.ppermute(v, 'img', core_pairs)]
    pallas_call x0 -> x2, Pallas kernels: none -> 85 us  [the longest x1 82.6 us: quick(): pl.pallas_call(reduce_body, in_specs=[vmem] * 12 + [hbm] * 3 + [vmem] * 3...]
    ppermute x60 -> x8, starting transfers between devices: 63.1 us -> 6.38 us  [the longest x2 3.22 us: hops(): lax.ppermute(parts[4], 'img', pairs[1])]
    dynamic_slice x22 -> x0, local copies, waits for them, and re-layouts: 19.9 us -> none  [the longest x12 10.7 us: halving_sum(): out = lax.dynamic_index_in_dim(v, 1 - bit, dim, keepdims=False)]
    convert_element_type x44 -> x0, other arithmetic: 12 us -> none  [halving_sum(): v = v.astype(BF)]
    slice x9 -> x0, local copies, waits for them, and re-layouts: 9.46 us -> none  [reduce_parts(): v[:, a:b]]
    ppermute x6 -> x8, waiting for transfers between devices: 8.12 us -> 13.7 us  [swap_lat(): return lax.ppermute(v, 'lat', [(0, 1), (1, 0)])]
    unnamed x51 -> x40, local copies, waits for them, and re-layouts: 2.88 us -> 6.91 us
  transfers between devices with their start and end apart: 66 -> 16, of which waited for: 36 -> 2; matrix products, arithmetic and copies ran while one was open for 11% -> 0% of each run, Pallas kernels for 10% -> 26%
where the time goes in v2:
time: 219 us; the launch traced here: 218 us
  Pallas kernels  176 us (80%)
  starting transfers between devices  16.1 us (7%)
  waiting for transfers between devices  13.7 us (6%)
  local copies, waits for them, and re-layouts  9.56 us (4%)
    pallas_call x11, Pallas kernels, call(): pl.pallas_call(body, grid=grid, in_specs=ins, out_specs=[o[1] for o in ou...  91.2 us
    pallas_call x1, Pallas kernels, quick(): pl.pallas_call(reduce_body, in_specs=[vmem] * 12 + [hbm] * 3 + [vmem] * 3...  82.6 us
    ppermute x8, waiting for transfers between devices, swap_lat(): return lax.ppermute(v, 'lat', [(0, 1), (1, 0)])  13.7 us
    ppermute x8, starting transfers between devices, swap_lat(): return lax.ppermute(v, 'lat', [(0, 1), (1, 0)])  9.74 us
    unnamed x40, local copies, waits for them, and re-layouts  6.91 us
  transfers between devices with their start and end apart: 16, of which 2 were waited for; matrix products, arithmetic and copies ran while one was open for 0% of the time, Pallas kernels for 26%

profile of v2, /device:TPU:0, one launch (start us, length us, event | category | flops | bytes accessed | tf_op | source)
XLA Modules:
  0.0 217.7 jit_solution(14600222665182926963)
XLA Ops:
  3.2 4.5 %shard_map.280 = (bf16[256,1024]{1,0:T(8,128)(2,1)}, bf16[256,512]{1,0:T(8,128)(2,1)}, bf16[256,1024]{1,0:T(8,128)(2,1)}) custom-call(s32[8]{0:T(128)} %stack.27.ints, bf16[256,1024]{1,0:T(8,128)(2,1)} %bitcast.44, bf16[256,1024]{1,0:T(8,128)(2,1)} %bitcast.51, f32[1,1024]{1,0:T(1,128)} %bitcast.60, f32[1,1024]{1,0:T(1,128)} %bitcast.62, bf16[1024,512]{1,0:T(8,128)(2,1)} %wq.3), custom_call_target="tpu_custom_call" | custom-call | flops 268435456 | bytes 3416096 | tf_op jit(solution)/shard_map/pallas_call | solution.py:36
  7.7 2.9 %collective-permute-start = (bf16[256,512]{1,0:T(8,128)(2,1)}, bf16[256,512]{1,0:T(8,128)(2,1)S(1)}, u32[]{:S(2)}, u32[]{:S(2)}) collective-permute-start(bf16[256,512]{1,0:T(8,128)(2,1)} %get-tuple-element.72.qo), channel_id=1, source_target_pairs={{0,1},{1,0},{2,3},{3,2},{4,5},{5,4},{6,7},{7,6},{8,9},{9,8},{10,11... | collective-permute-start | bytes 786440 | tf_op jit(solution)/shard_map/ppermute | solution.py:656
  10.6 7.6 %shard_map.281 = (bf16[1024,1024]{1,0:T(8,128)(2,1)}, bf16[1024,512]{1,0:T(8,128)(2,1)}, bf16[1024,512]{1,0:T(8,128)(2,1)}, bf16[256,512]{1,0:T(8,128)(2,1)}, bf16[256,512]{1,0:T(8,128)(2,1)}) custom-call(bf16[1024,1024]{1,0:T(8,128)(2,1)} %bitcast.65, f32[1,1024]{1,0:T(1,128)} %bitcast.70, f32[1,1024]{1,0:T(1,128)} %bitcast.68, bf16[1024,512]{1,0:T(8,128)(2,1)} %wk.5, ...), custom_call_target="tpu_custom_call" | custom-call | flops 2684354560 | bytes 9445376 | tf_op jit(solution)/shard_map/pallas_call | solution.py:36
  19.0 9.5 %shard_map.282 = (f32[256,512]{1,0:T(8,128)}, bf16[256,512]{1,0:T(8,128)(2,1)}, f32[256,128]{1,0:T(8,128)}, f32[256,128]{1,0:T(8,128)}) custom-call(bf16[256,512]{1,0:T(8,128)(2,1)} %get-tuple-element.72.qo, bf16[256,512]{1,0:T(8,128)(2,1)} %copy-done.14, bf16[1024,512]{1,0:T(8,128)(2,1)} %get-tuple-element.74.kp, bf16[1024,512]{1,0:T(8,128)(2,1)} %get-tuple-element.75.vp, ...), custom_call_target="tpu_custom_call" | custom-call | flops 1342177280 | bytes 4194304 | tf_op jit(solution)/shard_map/pallas_call | solution.py:36
  29.2 1.4 collective-permute-start.2
  30.6 8.8 %collective-permute-done.2.srecv = f32[256,128]{1,0:T(8,128)S(1)} collective-permute-done((f32[256,128]{1,0:T(8,128)}, f32[256,128]{1,0:T(8,128)S(1)}, u32[]{:S(2)}, u32[]{:S(2)}) %collective-permute-start.2) | collective-permute-done | bytes 131104 | tf_op jit(solution)/shard_map/ppermute | solution.py:656
  40.1 20.4 %shard_map.283 = (bf16[256,1024]{1,0:T(8,128)(2,1)}, bf16[2,2,2,2,128,256]{5,4,3,2,1,0:T(8,128)(2,1)}, bf16[2,2,2,2,128,256]{5,4,3,2,1,0:T(8,128)(2,1)}, bf16[25...) custom-call(s32[8]{0:T(128)} %stack.27.ints, ...), custom_call_target="tpu_custom_call" | custom-call | flops 8589934592 | bytes 27926560 | tf_op jit(solution)/shard_map/pallas_call | solution.py:36
  61.7 4.6 %shard_map.284 = (f32[256,1024]{1,0:T(8,128)}, bf16[256,512]{1,0:T(8,128)(2,1)}, f32[256,128]{1,0:T(8,128)}, bf16[2,2,2,2,2,16,1024]{6,5,4,3,2,1,0:T(8,128)(2,1)}, f32[2,1024]{1,0:T(2,128)}) custom-call(f32[256,1024]{1,0:T(8,128)} %get-tuple-element.84.residual, f32[256,1024]{1,0:T(8,128)} %get-tuple-element.85.gacc, ...), custom_call_target="tpu_custom_call" | custom-call | flops 536870912 | bytes 6828032 | tf_op jit(solution)/shard_map/pallas_call | solution.py:36
  66.8 1.5 collective-permute-start.4
  69.3 7.0 %shard_map.288 = (bf16[8,2,32,1024]{3,2,1,0:T(8,128)(2,1)}, bf16[8,2,32,1024]{3,2,1,0:T(8,128)(2,1)}, bf16[8,1,32,1024]{3,2,1,0:T(8,128)(2,1)}, bf16[8,1,32,1024...) custom-call(s32[8]{0:T(128)} %stack.27.ints, ...), custom_call_target="tpu_custom_call" | custom-call | flops 2147483648 | bytes 7340064 | tf_op jit(solution)/shard_map/pallas_call | solution.py:36
  76.8 1.6 collective-permute-start.12
  78.4 1.3 copy-done.8
  79.7 7.0 %shard_map.289 = (bf16[8,1,32,1024]{3,2,1,0:T(8,128)(2,1)}, bf16[8,1,32,1024]{3,2,1,0:T(8,128)(2,1)}, bf16[8,2,32,1024]{3,2,1,0:T(8,128)(2,1)}, bf16[8,2,32,1024...) custom-call(s32[8]{0:T(128)} %stack.27.ints, ...), custom_call_target="tpu_custom_call" | custom-call | flops 2147483648 | bytes 8912928 | tf_op jit(solution)/shard_map/pallas_call | solution.py:36
  88.6 10.1 %shard_map.285 = (bf16[1024,1024]{1,0:T(8,128)(2,1)}, bf16[256,1024]{1,0:T(8,128)(2,1)}, f32[256,512]{1,0:T(8,128)}, bf16[256,512]{1,0:T(8,128)(2,1)}) custom-call(bf16[256,512]{1,0:T(8,128)(2,1)} %get-tuple-element.72.qo, bf16[256,512]{1,0:T(8,128)(2,1)} %copy-done.14, bf16[1024,512]{1,0:T(8,128)(2,1)} %get-tuple-element.74.kp, ...), custom_call_target="tpu_custom_call" | custom-call | flops 3355443200 | bytes 7340032 | tf_op jit(solution)/shard_map/pallas_call | solution.py:36
  98.6 1.6 collective-permute-start.5
  100.2 1.6 collective-permute-start.14
  101.8 4.9 %collective-permute-done.5.drecv = bf16[256,512]{1,0:T(8,128)(2,1)S(1)} collective-permute-done((bf16[256,512]{1,0:T(8,128)(2,1)}, bf16[256,512]{1,0:T(8,128)(2,1)S(1)}, u32[]{:S(2)}, u32[]{:S(2)}) %collective-permute-start.5) | collective-permute-done | bytes 262176 | tf_op jit(solution)/shard_map/ppermute | solution.py:656
  107.3 1.6 collective-permute-start.15
  109.0 7.9 %shard_map.286 = (f32[1024,1024]{1,0:T(8,128)}, f32[2,1024]{1,0:T(2,128)}) custom-call(bf16[1024,1024]{1,0:T(8,128)(2,1)} %bitcast.66, bf16[1024,1024]{1,0:T(8,128)(2,1)} %get-tuple-element.90.dkvp, bf16[1024,512]{1,0:T(8,128)(2,1)} %wk.5, bf16[1024,512]{1,0:T(8,128)(2,1)} %wv.5, f32[1,1024]{1,0:T(1,128)} %bitcast.71), custom_call_target="tpu_custom_call" | custom-call | flops 2147483648 | bytes 10498048 | tf_op jit(solution)/shard_map/pallas_call | solution.py:36
  116.9 7.0 %shard_map.290 = bf16[1024,1024]{1,0:T(8,128)(2,1)} custom-call(bf16[1024,1024]{1,0:T(8,128)(2,1)} %get-tuple-element.114.media, bf16[256,1024]{1,0:T(8,128)(2,1)} %get-tuple-element.73.latent_norm.norm.latent, bf16[1024,1024]{1,0:T(8,128)(2,1)} %get-tuple-element.90.dkvp, bf16[256,1024]{1,0:T(8,128)(2,1)} %get-tuple-element.92.dkvl), custom_call_target="tpu_custom_call" | custom-call | flops 2684354560 | bytes 7340032 | tf_op jit(solution)/shard_map/pallas_call | solution.py:36
  123.8 5.6 %shard_map.287 = (f32[256,1024]{1,0:T(8,128)}, bf16[2,2,2,2,2,16,1024]{6,5,4,3,2,1,0:T(8,128)(2,1)}, f32[2,1024]{1,0:T(2,128)}) custom-call(bf16[256,1024]{1,0:T(8,128)(2,1)} %bitcast.46, bf16[256,1024]{1,0:T(8,128)(2,1)} %get-tuple-element.73.latent_norm.norm.latent, bf16[256,1024]{1,0:T(8,128)(2,1)} %get-tuple-element.92.dkvl, ...), custom_call_target="tpu_custom_call" | custom-call | flops 1073741824 | bytes 8663040 | tf_op jit(solution)/shard_map/pallas_call | solution.py:36
  131.3 82.6 %shard_map.291 = (f32[10,32,1024]{2,1,0:T(8,128)}, f32[8,1024]{1,0:T(8,128)}) custom-call(bf16[2,2,2,2,32,1024]{5,4,3,2,1,0:T(8,128)(2,1)} %bitcast.47, bf16[2,2,2,2,32,1024]{5,4,3,2,1,0:T(8,128)(2,1)} %bitcast.48, bf16[2,2,2,1,32,1024]{5,4,3,2,1,0:T(8,128)(2,1)} %bitcast.55, bf16[2,2,2,1,32,1024]{5,4,3,2,1,0:T(8,128)(2,1)} %bitcast.58, ...), custom_call_target="tpu_custom_call" | custom-call | tf_op jit(solution)/shard_map/pallas_call | solution.py:1267
  213.9 2.4 %shard_map.292 = (f32[32,4096]{1,0:T(8,128)}, f32[128,1024]{1,0:T(8,128)}, f32[32,512]{1,0:T(8,128)}, f32[32,512]{1,0:T(8,128)}, f32[16,1024]{1,0:T(8,128)}, /*index=5*/f32[32,512]{1,0:T(8,128)}, f32[8,128]{1,0:T(8,128)}) custom-call(s32[8]{0:T(128)} %stack.27.ints, f32[10,32,1024]{2,1,0:T(8,128)} %get-tuple-element.120.fin, f32[8,1024]{1,0:T(8,128)} %get-tuple-element.121.vec), custom_call_target="tpu_custom_call" | custom-call | tf_op jit(solution)/shard_map/pallas_call | solution.py:1294
  216.3 1.4 slice_bitcast_fusion
  (64 shorter events, 12.0 us)
Async XLA Ops:
  7.7 10.5 %collective-permute-start = (bf16[256,512]{1,0:T(8,128)(2,1)}, bf16[256,512]{1,0:T(8,128)(2,1)S(1)}, u32[]{:S(2)}, u32[]{:S(2)}) collective-permute-start(bf16[256,512]{1,0:T(8,128)(2,1)} %get-tuple-element.72.qo), channel_id=1, source_target_pairs={{0,1},{1,0},{2,3},{3,2},{4,5},{5,4},{6,7},{7,6},{8,9},{9,8},{10,11... | collective-permute-start | bytes 786440 | tf_op jit(solution)/shard_map/ppermute | solution.py:656
  28.5 10.9 %collective-permute-start.1 = (bf16[256,512]{1,0:T(8,128)(2,1)}, bf16[256,512]{1,0:T(8,128)(2,1)S(1)}, u32[]{:S(2)}, u32[]{:S(2)}) collective-permute-start(bf16[256,512]{1,0:T(8,128)(2,1)} %get-tuple-element.79), channel_id=1, source_target_pairs={{0,1},{1,0},{2,3},{3,2},{4,5},{5,4},{6,7},{7,6},{8,9},{9,8},{10,11... | collective-permute-start | bytes 786440 | tf_op jit(solution)/shard_map/ppermute | solution.py:656
  29.2 10.1 %collective-permute-start.2 = (f32[256,128]{1,0:T(8,128)}, f32[256,128]{1,0:T(8,128)S(1)}, u32[]{:S(2)}, u32[]{:S(2)}) collective-permute-start(f32[256,128]{1,0:T(8,128)} %get-tuple-element.81), channel_id=1, source_target_pairs={{0,1},{1,0},{2,3},{3,2},{4,5},{5,4},{6,7},{7,6},{8,9},{9,8},{10,11... | collective-permute-start | bytes 393224 | tf_op jit(solution)/shard_map/ppermute | solution.py:656
  40.1 21.0 %copy-start.2 = (bf16[256,1024]{1,0:T(8,128)(2,1)S(1)}, bf16[256,1024]{1,0:T(8,128)(2,1)}, u32[]{:S(2)}) copy-start(bf16[256,1024]{1,0:T(8,128)(2,1)} %get-tuple-element.82.og) | copy-start | bytes 1572868
  60.6 17.8 %collective-permute-start.10 = (bf16[256,4096]{1,0:T(8,128)(2,1)}, bf16[256,4096]{1,0:T(8,128)(2,1)S(1)}, u32[]{:S(2)}, u32[]{:S(2)}) collective-permute-start(bf16[256,4096]{1,0:T(8,128)(2,1)} %get-tuple-element.103.pre), channel_id=1, source_target_pairs={{0,2},{2,0},{4,6},{6,4},{8,10},{10,8},{12,14},{14,12},{16,18},{18,... | collective-permute-start | bytes 6291464 | tf_op jit(solution)/shard_map/ppermute | solution.py:1007
  60.7 7.7 %collective-permute-start.6 = (bf16[2,2,2,2,128,256]{5,4,3,2,1,0:T(8,128)(2,1)}, bf16[2,2,2,2,128,256]{5,4,3,2,1,0:T(8,128)(2,1)S(1)}, u32[]{:S(2)}, u32[]{:S(2)}) collective-permute-start(bf16[2,2,2,2,128,256]{5,4,3,2,1,0:T(8,128)(2,1)} %get-tuple-element.98), channel_id=1, source_target_pairs={{0,2},{2,0},{4,6},{6,4},{8,10},{10,8},{12,14},{14,12},{16,18},{18,... | collective-permute-start | bytes 3145736 | tf_op jit(solution)/shard_map/ppermute | solution.py:1007
  61.2 5.6 %collective-permute-start.7 = (bf16[256,1024]{1,0:T(8,128)(2,1)S(1)}, bf16[256,1024]{1,0:T(8,128)(2,1)S(1)}, u32[]{:S(2)}, u32[]{:S(2)}) collective-permute-start(bf16[256,1024]{1,0:T(8,128)(2,1)S(1)} %copy-done.2), channel_id=1, source_target_pairs={{0,2},{2,0},{4,6},{6,4},{8,10},{10,8},{12,14},{14,12},{16,18},{18,... | collective-permute-start | bytes 1572872 | tf_op jit(solution)/shard_map/ppermute | solution.py:1007
  61.2 15.6 %collective-permute-start.9 = (bf16[2,2,2,2,32,256]{5,4,3,2,1,0:T(8,128)(2,1)}, bf16[2,2,2,2,32,256]{5,4,3,2,1,0:T(8,128)(2,1)S(1)}, u32[]{:S(2)}, u32[]{:S(2)}) collective-permute-start(bf16[2,2,2,2,32,256]{5,4,3,2,1,0:T(8,128)(2,1)} %get-tuple-element.102), channel_id=1, source_target_pairs={{0,2},{2,0},{4,6},{6,4},{8,10},{10,8},{12,14},{14,12},{16,18},{18,... | collective-permute-start | bytes 786440 | tf_op jit(solution)/shard_map/ppermute | solution.py:1007
  66.3 20.9 %collective-permute-start.3 = (bf16[256,512]{1,0:T(8,128)(2,1)}, bf16[256,512]{1,0:T(8,128)(2,1)S(1)}, u32[]{:S(2)}, u32[]{:S(2)}) collective-permute-start(bf16[256,512]{1,0:T(8,128)(2,1)} %get-tuple-element.88.do), channel_id=1, source_target_pairs={{0,1},{1,0},{2,3},{3,2},{4,5},{5,4},{6,7},{7,6},{8,9},{9,8},{10,11... | collective-permute-start | bytes 786440 | tf_op jit(solution)/shard_map/ppermute | solution.py:656
  66.8 20.4 %collective-permute-start.4 = (f32[256,128]{1,0:T(8,128)}, f32[256,128]{1,0:T(8,128)S(1)}, u32[]{:S(2)}, u32[]{:S(2)}) collective-permute-start(f32[256,128]{1,0:T(8,128)} %get-tuple-element.89.so), channel_id=1, source_target_pairs={{0,1},{1,0},{2,3},{3,2},{4,5},{5,4},{6,7},{7,6},{8,9},{9,8},{10,11... | collective-permute-start | bytes 393224 | tf_op jit(solution)/shard_map/ppermute | solution.py:656
  76.3 53.2 %collective-permute-start.8 = (bf16[8,2,32,1024]{3,2,1,0:T(8,128)(2,1)}, bf16[8,2,32,1024]{3,2,1,0:T(8,128)(2,1)S(1)}, u32[]{:S(2)}, u32[]{:S(2)}) collective-permute-start(bf16[8,2,32,1024]{3,2,1,0:T(8,128)(2,1)} %get-tuple-element.100), channel_id=1, source_target_pairs={{0,1},{1,0},{2,3},{3,2},{4,5},{5,4},{6,7},{7,6},{8,9},{9,8},{10,11... | collective-permute-start | bytes 3145736 | tf_op jit(solution)/shard_map/ppermute | solution.py:656
  76.8 1.6 copy-start.16
  76.8 30.5 %collective-permute-start.12 = (bf16[8,1,32,1024]{3,2,1,0:T(8,128)(2,1)}, bf16[8,1,32,1024]{3,2,1,0:T(8,128)(2,1)S(1)}, u32[]{:S(2)}, u32[]{:S(2)}) collective-permute-start(bf16[8,1,32,1024]{3,2,1,0:T(8,128)(2,1)} %get-tuple-element.107), channel_id=1, source_target_pairs={{0,4},{2,6},{4,0},{6,2},{8,12},{10,14},{12,8},{14,10},{16,20},{18,... | collective-permute-start | bytes 1572872 | tf_op jit(solution)/shard_map/ppermute | solution.py:1152
  86.6 13.6 %copy-start.10 = (bf16[8,1,32,1024]{3,2,1,0:T(8,128)(2,1)S(1)}, bf16[8,1,32,1024]{3,2,1,0:T(8,128)(2,1)}, u32[]{:S(2)}) copy-start(bf16[8,1,32,1024]{3,2,1,0:T(8,128)(2,1)} %get-tuple-element.111) | copy-start | bytes 1572868
  86.7 20.1 %copy-start.12 = (bf16[8,1,32,1024]{3,2,1,0:T(8,128)(2,1)S(1)}, bf16[8,1,32,1024]{3,2,1,0:T(8,128)(2,1)}, u32[]{:S(2)}) copy-start(bf16[8,1,32,1024]{3,2,1,0:T(8,128)(2,1)} %get-tuple-element.105) | copy-start | bytes 1572868
  86.7 20.7 %copy-start.11 = (bf16[8,1,32,1024]{3,2,1,0:T(8,128)(2,1)S(1)}, bf16[8,1,32,1024]{3,2,1,0:T(8,128)(2,1)}, u32[]{:S(2)}) copy-start(bf16[8,1,32,1024]{3,2,1,0:T(8,128)(2,1)} %get-tuple-element.113) | copy-start | bytes 1572868
  86.7 42.8 %collective-permute-start.13 = (bf16[8,2,32,1024]{3,2,1,0:T(8,128)(2,1)}, bf16[8,2,32,1024]{3,2,1,0:T(8,128)(2,1)S(1)}, u32[]{:S(2)}, u32[]{:S(2)}) collective-permute-start(bf16[8,2,32,1024]{3,2,1,0:T(8,128)(2,1)} %get-tuple-element.109), channel_id=1, source_target_pairs={{0,4},{2,6},{4,0},{6,2},{8,12},{10,14},{12,8},{14,10},{16,20},{18,... | collective-permute-start | bytes 3145736 | tf_op jit(solution)/shard_map/ppermute | solution.py:1152
  98.6 8.1 %collective-permute-start.5 = (bf16[256,512]{1,0:T(8,128)(2,1)}, bf16[256,512]{1,0:T(8,128)(2,1)S(1)}, u32[]{:S(2)}, u32[]{:S(2)}) collective-permute-start(bf16[256,512]{1,0:T(8,128)(2,1)} %get-tuple-element.94), channel_id=1, source_target_pairs={{0,1},{1,0},{2,3},{3,2},{4,5},{5,4},{6,7},{7,6},{8,9},{9,8},{10,11... | collective-permute-start | bytes 786440 | tf_op jit(solution)/shard_map/ppermute | solution.py:656
  100.2 29.2 %collective-permute-start.14 = (bf16[8,1,32,1024]{3,2,1,0:T(8,128)(2,1)S(1)}, bf16[8,1,32,1024]{3,2,1,0:T(8,128)(2,1)S(1)}, u32[]{:S(2)}, u32[]{:S(2)}) collective-permute-start(bf16[8,1,32,1024]{3,2,1,0:T(8,128)(2,1)S(1)} %copy-done.10), channel_id=1, source_target_pairs={{0,8},{2,10},{4,12},{6,14},{8,0},{10,2},{12,4},{14,6},{16,24},{18,... | collective-permute-start | bytes 1572872 | tf_op jit(solution)/shard_map/ppermute | solution.py:1154
  106.7 10.1 %copy-start.7 = (bf16[256,512]{1,0:T(8,128)(2,1)}, bf16[256,512]{1,0:T(8,128)(2,1)S(1)}, u32[]{:S(2)}) copy-start(bf16[256,512]{1,0:T(8,128)(2,1)S(1)} %collective-permute-done.5.drecv) | copy-start | bytes 786436
  106.7 22.8 %collective-permute-start.11 = (bf16[8,1,32,1024]{3,2,1,0:T(8,128)(2,1)S(1)}, bf16[8,1,32,1024]{3,2,1,0:T(8,128)(2,1)S(1)}, u32[]{:S(2)}, u32[]{:S(2)}) collective-permute-start(bf16[8,1,32,1024]{3,2,1,0:T(8,128)(2,1)S(1)} %copy-done.12), channel_id=1, source_target_pairs={{0,1},{1,0},{2,3},{3,2},{4,5},{5,4},{6,7},{7,6},{8,9},{9,8},{10,11... | collective-permute-start | bytes 1572872 | tf_op jit(solution)/shard_map/ppermute | solution.py:656
  107.3 9.5 %copy-start.3 = (bf16[8,1,32,1024]{3,2,1,0:T(8,128)(2,1)}, bf16[8,1,32,1024]{3,2,1,0:T(8,128)(2,1)S(1)}, u32[]{:S(2)}) copy-start(bf16[8,1,32,1024]{3,2,1,0:T(8,128)(2,1)S(1)} %collective-permute-done.12) | copy-start | bytes 1572868
  107.3 22.2 %collective-permute-start.15 = (bf16[8,1,32,1024]{3,2,1,0:T(8,128)(2,1)S(1)}, bf16[8,1,32,1024]{3,2,1,0:T(8,128)(2,1)S(1)}, u32[]{:S(2)}, u32[]{:S(2)}) collective-permute-start(bf16[8,1,32,1024]{3,2,1,0:T(8,128)(2,1)S(1)} %copy-done.11), channel_id=1, source_target_pairs={{0,8},{2,10},{4,12},{6,14},{8,0},{10,2},{12,4},{14,6},{16,24},{18,... | collective-permute-start | bytes 1572872 | tf_op jit(solution)/shard_map/ppermute | solution.py:1154
  129.5 1.8 copy-start.1
  (12 other events, 11.9 us)

commit v3 on v1

--- a/solution.py
+++ b/solution.py
@@ -1,4 +1,5 @@
 from functools import partial
+from types import SimpleNamespace
 
 import jax
 import jax.numpy as jnp
@@ -304,13 +305,594 @@
     latent, norm, dkvl, dqo, drecv, residual_grad, wq, wk, wv, gain, out, query_grad, vectors
 ):
     dq = (dqo[...] + drecv[...].astype(F32)).astype(BF)
-    query_grad[...] = (HEAD_DIM**-0.5 * t_dot(norm[...], dq)).astype(BF)
+    product = (HEAD_DIM**-0.5 * t_dot(norm[...], dq)).astype(BF)
+    if query_grad.shape == product.shape:
+        query_grad[...] = product
+    else:
+        product = product.reshape(-1, 32, INNER)
+        shape = query_grad.shape[:-1] + (INNER,)
+        query_grad[..., :INNER] = product[:, :16].reshape(shape)
+        query_grad[..., INNER:] = product[:, 16:].reshape(shape)
     grad = dot_t(dkvl[:, :INNER], wk[...]) + dot_t(dkvl[:, INNER:], wv[...])
     grad += HEAD_DIM**-0.5 * dot_t(dq, wq[...])
     unit, scale = centred(latent[...].astype(F32))
     vectors[0:1, :] = column_sum(grad * unit)
     vectors[1:2, :] = column_sum(grad)
     out[...] = residual_grad[...] + norm_back(unit, scale, gain[...], grad)
+
+
+def ffn_back_body(
+    residual, gacc, og, mix_ref, packed, wo, gain, residual_grad, attended_grad, stats, out, vectors
+):
+    unit, scale = centred(residual[...])
+    grad = gacc[...]
+    vectors[0:1, :] = column_sum(grad * unit)
+    vectors[1:2, :] = column_sum(grad)
+    res_grad = og[...].astype(F32) + norm_back(unit, scale, gain[...], grad)
+    residual_grad[...] = res_grad
+    branch = res_grad.astype(BF)
+    back = dot_t(branch, wo[...]).astype(BF)
+    attended_grad[...] = back
+    mix = mix_ref[...]
+    product = back.astype(F32) * mix
+    head = head_of(product.shape)
+    sums = [
+        jnp.sum(jnp.where(head == h, product, 0.0), axis=-1, keepdims=True) for h in range(HEADS)
+    ]
+    delta = pack_lanes(sums)
+    lane = lax.broadcasted_iota(jnp.int32, delta.shape, 1)
+    stats[...] = jnp.where(lane % PER < PER // 2, packed[...], delta)
+    if out is not None:
+        out[...] = t_dot(mix.astype(BF), branch).astype(BF).reshape(out.shape)
+
+
+def plus(a, b):
+    return a.astype(F32) + b.astype(F32)
+
+
+class Names:
+    def __getattr__(self, name):
+        return name
+
+
+n = Names()
+STREAMS = ("d0", "d1", "d2", "d3", "u0", "u1", "u2", "u3", "K", "W", "Q")
+ORDERS = {
+    "d0": "ywxz", "d1": "zwyx", "d2": "yxzw", "d3": "yxzw", "u0": "yzwx", "u1": "yxzw",
+    "u2": "xyzw", "u3": "zxyw", "K": "wxyz", "W": "yzxw", "Q": "xywz",
+}
+PLAN = (
+    "fi", "md0", "md1", "md2", "md3", "af0:4", "af4:8", "cb", "j0", "j1", "j2", "j3", "u0", "j4", "j5", "u1", "j6", "j7", "fb", "+u0", "u2", "d0",
+    "d1", "d2", "d3", "+u0", "u3", "+u1", "at0:5", "+u0", "at5:7", "+d1", "at7:8", "+d0", "+u2",
+    "kv0", "kv1", "kv2", "+u1", "kv3", "+u0", "ow", "+d2", "+K", "+u3", "+W", "+d1", "lat",
+    "pt0", "+d2", "pt1", "+Q", "+d3", "pt2", "+d0", "+u3", "pt3", "+u1", "+u2", "+V", "+W",
+    "+d2", "+K", "+d1", "+Q", "+u1", "+u3", "+u2", "+d2", "+d3", "+W", "+u3", "+Q", "+d0", "+V",
+    "+u2", "+K", "+V", "+d3", "+d1", "+W", "+K", "+Q", "+d0", "+V", "+d3", "+W", "+K", "+V",
+    "+Q",
+)
+DIMS = "wzyx"
+DIMS_ALL = "wzycx"
+BLOCK = (32, 1024)
+LOADED = (n.latent, n.wq, n.og, n.patch, n.wo)
+GIVEN = LOADED + (
+    n.wk, n.wv, n.wup, n.wdown, n.images, n.device, n.fg, n.fb, n.mg, n.mb, n.lg, n.lb,
+)
+
+
+def is_late(s):
+    return s in "KWQ"
+
+
+def main_scratch(nl, np_, width, hidden):
+    def bf(*shape):
+        return pltpu.VMEM(shape, BF)
+
+    def f4(*shape):
+        return pltpu.VMEM(shape, F32)
+
+    step = hidden // 8
+    turned = (2, 2, 2, 2, step // 4, nl)
+    turned_in = (2, 2, 2, 2, 32, nl)
+    items = [
+        (n.latent, bf(nl, width)),
+        (n.wq, bf(width, INNER)),
+        (n.og, bf(nl, width)),
+        (n.patch, bf(np_, width)),
+        (n.wo, bf(INNER, width)),
+        (n.oo, f4(nl, INNER)),
+        (n.op, bf(nl, INNER)),
+        (n.so, f4(nl, LANES)),
+        (n.sp, f4(nl, LANES)),
+        (n.orecv, bf(nl, INNER)),
+        (n.srecv, f4(nl, LANES)),
+        (n.q, bf(nl, INNER)),
+        (n.q_peer, bf(nl, INNER)),
+        (n.kp, bf(np_, INNER)),
+        (n.vp, bf(np_, INNER)),
+        (n.kl, bf(nl, INNER)),
+        (n.vl, bf(nl, INNER)),
+        (n.norm_l, bf(nl, width)),
+        (n.norm_m, bf(np_, width)),
+        (n.wu, bf(2, width, step)),
+        (n.wd, bf(2, step, width)),
+        (n.og_sib, bf(nl, width)),
+        (n.act_own, bf(*turned)),
+        (n.act_send, bf(*turned)),
+        (n.act_sib, bf(*turned)),
+        (n.ffn_own, bf(*turned_in)),
+        (n.ffn_send, bf(*turned_in)),
+        (n.ffn_sib, bf(*turned_in)),
+        (n.residual, f4(nl, width)),
+        (n.gacc, f4(nl, width)),
+        (n.acc, f4(nl, width)),
+        (n.ffn_in, bf(nl, width)),
+        (n.attended, f4(nl, INNER)),
+        (n.packed, f4(nl, LANES)),
+        (n.fresh, bf(nl, width)),
+        (n.grad, bf(nl, INNER)),
+        (n.stats, f4(nl, LANES)),
+        (n.grad_peer, bf(nl, INNER)),
+        (n.stats_peer, f4(nl, LANES)),
+        (n.dkvp, bf(np_, 2 * INNER)),
+        (n.dkvl, bf(nl, 2 * INNER)),
+        (n.dq_peer, bf(nl, INNER)),
+        (n.vs, f4(5, 8, width)),
+        (n.vr, f4(5, 8, width)),
+        (n.sums, f4(2, width)),
+        (n.pre, bf(2, 2, 2, 2, 2, *BLOCK)),
+        (n.pre_sib, bf(2, 2, 2, 2, 2, *BLOCK)),
+    ]
+    items += [(s, bf(2, 2, 2, 2, *BLOCK)) for s in STREAMS if not is_late(s)]
+    for s in STREAMS:
+        wide = BLOCK[1] // 2 if s in "KW" else BLOCK[1]
+        for k in range(4 if is_late(s) else 3, -1, -1):
+            items.append((s + "_%d" % k, bf(*((2,) * k), BLOCK[0], wide)))
+    dma = pltpu.SemaphoreType.DMA
+    items += [
+        (n.load_sem, dma((len(LOADED) + 4,))),
+        (n.weight_sem, dma((2, 2))),
+        (n.store_sem, dma((6,))),
+        (n.send_sem, dma((80,))),
+        (n.recv_sem, dma((80,))),
+    ]
+    return [k for k, _ in items], [v for _, v in items]
+
+
+def main_body(names, *refs):
+    src = SimpleNamespace(**dict(zip(GIVEN, refs)))
+    outs = len(GIVEN)
+    fin, vec, patches_low, latents_grad, new_latents = refs[outs : outs + 5]
+    t = SimpleNamespace(**dict(zip(names, refs[outs + 5 :])))
+    load_sem, weight_sem, store_sem = t.load_sem, t.weight_sem, t.store_sem
+    mine = lax.axis_index("img")
+    xb = lax.axis_index("lat")
+    bit = {"x": xb, "c": mine % 2, "y": (mine // 2) % 2, "z": (mine // 4) % 2, "w": (mine // 8) % 2}
+
+    def to(axis, weight):
+        return (mine + weight - 2 * weight * bit[axis], xb)
+
+    peer = {"c": to("c", 1), "y": to("y", 2), "z": to("z", 4), "w": to("w", 8), "x": (mine, 1 - xb)}
+    barrier = pltpu.get_barrier_semaphore()
+    for axis in peer:
+        pl.semaphore_signal(
+            barrier, inc=1, device_id=peer[axis], device_id_type=pl.DeviceIdType.MESH
+        )
+
+    step = t.wd.shape[1]
+    count = t.og.shape[0]
+    weights = {}
+
+    def load_weights(j):
+        slot = j % 2
+        col = pl.ds(j * step, step)
+        pair = (
+            pltpu.make_async_copy(src.wup.at[:, col], t.wu.at[slot], weight_sem.at[0, slot]),
+            pltpu.make_async_copy(src.wdown.at[col], t.wd.at[slot], weight_sem.at[1, slot]),
+        )
+        for copy in pair:
+            copy.start()
+        weights[j] = pair
+
+    loads = {}
+
+    def load(names):
+        for name in names:
+            i = LOADED.index(name)
+            loads[name] = pltpu.make_async_copy(getattr(src, name), getattr(t, name), load_sem.at[i])
+            loads[name].start()
+
+    def load_kv(first):
+        for i, name in enumerate((n.wk, n.wv)):
+            loads[name] = pltpu.make_async_copy(
+                getattr(src, name), t.wu.at[i], load_sem.at[len(LOADED) + first + i]
+            )
+            loads[name].start()
+
+    load(LOADED[:3])
+    load_kv(0)
+    load(LOADED[3:])
+
+    def need(*names):
+        for name in names:
+            if name in loads:
+                loads.pop(name).wait()
+
+    pl.semaphore_wait(barrier, len(peer))
+    used = []
+
+    def send(source, target, axis):
+        slot = len(used)
+        copy = pltpu.make_async_remote_copy(
+            src_ref=source,
+            dst_ref=target,
+            send_sem=t.send_sem.at[slot],
+            recv_sem=t.recv_sem.at[slot],
+            device_id=peer[axis],
+            device_id_type=pl.DeviceIdType.MESH,
+        )
+        copy.start()
+        used.append(copy)
+        return copy
+
+    arriving = {}
+
+    def arrive(*names):
+        for name in names:
+            if name in arriving:
+                arriving.pop(name).wait_recv()
+
+    order = {s: ("c" if is_late(s) else "") + ORDERS[s] for s in STREAMS}
+    place = {s: 0 for s in STREAMS}
+    half = BLOCK[1] // 2
+    buffer = {s: getattr(t, s) for s in STREAMS if not is_late(s)}
+    buffer["K"] = buffer["W"] = t.pre
+    buffer["Q"] = t.pre_sib
+    column = {"K": pl.ds(0, half), "W": pl.ds(half, half)}
+
+    def where(s, axis, value):
+        done = order[s][: place[s]]
+        index = []
+        for d in DIMS_ALL if is_late(s) else DIMS:
+            if d == axis:
+                index.append(value)
+            else:
+                index.append(bit[d] if d in done else slice(None))
+        if s in column:
+            index += [slice(None), column[s]]
+        return tuple(index)
+
+    def got(s):
+        return getattr(t, s + "_%d" % (len(order[s]) - 1 - place[s]))
+
+    def start(s):
+        axis = order[s][place[s]]
+        arriving[s] = send(buffer[s].at[where(s, axis, 1 - bit[axis])], got(s), axis)
+
+    def take(s):
+        axis = order[s][place[s]]
+        arrive(s)
+        if s == "Q" and place[s] == 0:
+            arrive(n.O)
+        at = where(s, axis, bit[axis])
+        total = plus(buffer[s][at], got(s)[...])
+        place[s] += 1
+        if place[s] < len(order[s]):
+            buffer[s][at] = total.astype(BF)
+            start(s)
+        elif s in column:
+            fin[8, :, column[s]] = total
+        else:
+            fin[9 if s == "Q" else STREAMS.index(s)] = total
+
+    vs, vr = t.vs, t.vr
+    vec_order = "cxyzw"
+    vec_place = [0]
+
+    def take_vector():
+        i = vec_place[0]
+        arrive(n.V)
+        if i < 4:
+            vs[i + 1] = vs[i] + vr[i]
+            arriving["V"] = send(vs.at[i + 1], vr.at[i + 1], vec_order[i + 1])
+        else:
+            vec[...] = vs[i] + vr[i]
+        vec_place[0] += 1
+
+    stores = []
+
+    def store(source, target):
+        stores.append(pltpu.make_async_copy(source, target, store_sem.at[len(stores)]))
+        stores[-1].start()
+
+    core = bit["c"]
+    size = t.patch.shape[0] // 4
+
+    def live_rows():
+        total = jnp.int32(0)
+        for i in range(src.images.shape[0]):
+            total += jnp.where(src.device[i] == mine, src.images[i], 0)
+        slot = lax.broadcasted_iota(jnp.int32, (count, 1), 0) // (count // 8)
+        return jnp.where(slot < total, 1.0, 0.0).astype(F32)
+
+    def first():
+        need(n.latent, n.wq)
+        unit, _ = centred(t.latent[...].astype(F32))
+        low = (unit * src.lg[...] + src.lb[...]).astype(BF)
+        t.norm_l[...] = low
+        t.q[...] = (HEAD_DIM**-0.5 * dot(low, t.wq[...])).astype(BF)
+        arriving[n.q_peer] = send(t.q, t.q_peer, "x")
+        need(n.og, n.wk, n.wv)
+        t.og[...] = (t.og[...].astype(F32) * live_rows()).astype(BF)
+        arriving[n.og_sib] = send(t.og, t.og_sib, "c")
+        t.kl[...] = dot(low, t.wu[0]).astype(BF)
+        t.vl[...] = dot(low, t.wu[1]).astype(BF)
+
+    def media(i):
+        need(n.patch)
+        at = pl.ds(i * size, size)
+        unit, _ = centred(t.patch[at].astype(F32))
+        low = (unit * src.mg[...] + src.mb[...]).astype(BF)
+        t.norm_m[at] = low
+        t.kp[at] = dot(low, t.wu[0]).astype(BF)
+        t.vp[at] = dot(low, t.wu[1]).astype(BF)
+        if i == 3:
+            load_weights(0)
+            load_weights(1)
+
+    def slot_rows(i):
+        lat, med = count // 8, t.kp.shape[0] // 8
+        return (
+            pl.ds(pl.multiple_of(i * lat, lat), lat),
+            pl.ds(pl.multiple_of(i * med, med), med),
+        )
+
+    def attend(first, last):
+        arrive(n.q_peer)
+
+        @pl.loop(first, last)
+        def _(i):
+            a, b = slot_rows(i)
+            attend_body(
+                t.q.at[a], t.q_peer.at[a], t.kp.at[b], t.vp.at[b], t.kl.at[a], t.vl.at[a],
+                t.oo.at[a], t.op.at[a], t.so.at[a], t.sp.at[a],
+            )
+
+        at = pl.ds(first * (count // 8), (last - first) * (count // 8))
+        arriving["o%d" % first] = send(t.op.at[at], t.orecv.at[at], "x")
+        arriving["s%d" % first] = send(t.sp.at[at], t.srecv.at[at], "x")
+
+    def combine():
+        need(n.wo)
+        for name in list(arriving):
+            if name[0] in "os" and name[1:].isdigit():
+                arrive(name)
+        a, b = t.so[...], t.srecv[...]
+        top = jnp.maximum(a, b)
+        both = top + jnp.log(jnp.exp(a - top) + jnp.exp(b - top))
+        t.packed[...] = both
+        mix = widen(jnp.exp(a - both)) * t.oo[...]
+        mix += widen(jnp.exp(b - both)) * t.orecv[...].astype(F32)
+        t.attended[...] = mix
+        res = t.latent[...].astype(F32) + dot(mix.astype(BF), t.wo[...])
+        t.residual[...] = res
+        unit, _ = centred(res)
+        low = (unit * src.fg[...] + src.fb[...]).astype(BF)
+        t.ffn_in[...] = low
+        turned = low.T.reshape(8, 2, -1, count)
+        even, odd = turned[:, 0], turned[:, 1]
+        shape = t.ffn_own.shape
+        t.ffn_own[...] = jnp.where(core == 0, even, odd).reshape(shape)
+        t.ffn_send[...] = jnp.where(core == 0, odd, even).reshape(shape)
+        arriving[n.ffn_sib] = send(t.ffn_send, t.ffn_sib, "c")
+
+    def ffn(j):
+        for copy in weights.pop(j):
+            copy.wait()
+        wup, wdown = t.wu[j % 2], t.wd[j % 2]
+        pre = dot(t.ffn_in[...], wup)
+        cdf = 0.5 * (1.0 + lax.erf(pre * (0.5**0.5)))
+        act = (pre * cdf).astype(BF)
+        turned = act.T
+        even, odd = turned[: step // 2], turned[step // 2 :]
+        at = (j // 4, (j // 2) % 2, j % 2)
+        shape = t.act_own.shape[3:]
+        t.act_own[at] = jnp.where(core == 0, even, odd).reshape(shape)
+        t.act_send[at] = jnp.where(core == 0, odd, even).reshape(shape)
+        arriving["act%d" % j] = send(t.act_send.at[at], t.act_sib.at[at], "c")
+        down = dot(act, wdown)
+        act_grad = dot_t(t.og[...], wdown)
+        pdf = jnp.exp(-0.5 * pre * pre) * 0.3989422804014327
+        pre_grad = (act_grad * (cdf + pre * pdf)).astype(BF)
+        group = (j // 4, (j // 2) % 2)
+        t.pre[group + (slice(None),) * 4 + (pl.ds((j % 2) * step, step),)] = pre_grad.reshape(
+            2, 2, 2, 32, step
+        )
+        if j % 2 == 1:
+            name = "pre%d" % (j // 2)
+            arriving[name] = send(t.pre.at[group], t.pre_sib.at[group], "c")
+            pre_sent.append(len(used) - 1)
+        back = dot_t(pre_grad, wup)
+        if j == 0:
+            t.acc[...] = down
+            t.gacc[...] = back
+        else:
+            t.acc[...] += down
+            t.gacc[...] += back
+        if j < 6:
+            load_weights(j + 2)
+        if j == 7:
+            load_kv(2)
+            t.fresh[...] = ((t.residual[...] + t.acc[...]) * live_rows()).astype(BF)
+            store(t.fresh, new_latents)
+
+    pre_sent = []
+
+    def ffn_back():
+        ffn_back_body(
+            t.residual, t.gacc, t.og, t.attended, t.packed, t.wo, src.fg,
+            t.residual, t.grad, t.stats, None, vs.at[0, pl.ds(4, 2)],
+        )
+        arriving[n.grad_peer] = send(t.grad, t.grad_peer, "x")
+        arriving[n.stats_peer] = send(t.stats, t.stats_peer, "x")
+
+    def send_late(rows, name):
+        o, r = buffer["Q"], t.Q_4
+        arriving[name] = send(
+            o.at[:, :, :, 1 - core, :, rows], r.at[:, :, :, :, rows], "c"
+        )
+
+    def output_group():
+        product = t_dot(t.attended[...].astype(BF), t.residual[...].astype(BF)).astype(BF)
+        buffer["Q"][..., pl.ds(0, 16), :] = product.reshape(2, 2, 2, 2, 2, 16, BLOCK[1])
+        send_late(pl.ds(0, 16), "O")
+
+    def rows_of(ref, at):
+        v = ref[at]
+        return v.reshape(-1, v.shape[-1])
+
+    def down_group(g):
+        s = "d%d" % g
+        arrive(n.og_sib, *("act%d" % j for j in range(8)))
+        axis = order[s][0]
+        col = pl.ds(g * 256, 256)
+        for value in (1 - bit[axis], bit[axis]):
+            at = where(s, axis, value)
+            v = dot(rows_of(t.act_own, at), t.og[:, col])
+            v += dot(rows_of(t.act_sib, at), t.og_sib[:, col])
+            v = v.astype(BF).reshape(2, 2, 2, 4, 32, 256)
+            for k in range(4):
+                buffer[s][at + (slice(None), pl.ds(k * 256, 256))] = v[:, :, :, k]
+            if s not in arriving:
+                start(s)
+
+    def up_group(g):
+        s = "u%d" % g
+        arrive(n.ffn_sib, "pre%d" % g)
+        axis = order[s][0]
+        group = (g // 2, g % 2)
+        for value in (1 - bit[axis], bit[axis]):
+            at = where(s, axis, value)
+            v = dot(rows_of(t.ffn_own, at), rows_of(t.pre, group))
+            v += dot(rows_of(t.ffn_sib, at), rows_of(t.pre_sib, group))
+            buffer[s][at] = v.astype(BF).reshape((2, 2, 2) + BLOCK)
+            if s not in arriving:
+                start(s)
+
+    def attend_back(first, last):
+        arrive(n.grad_peer, n.stats_peer)
+
+        @pl.loop(first, last)
+        def _(i):
+            a, b = slot_rows(i)
+            attend_back_body(
+                t.q.at[a], t.q_peer.at[a], t.kp.at[b], t.vp.at[b], t.kl.at[a],
+                t.vl.at[a], t.grad.at[a], t.grad_peer.at[a], t.stats.at[a],
+                t.stats_peer.at[a], t.dkvp.at[b], t.dkvl.at[a], t.oo.at[a],
+                t.dq_peer.at[a],
+            )
+
+        if last == 8:
+            arriving[n.dq_recv] = send(t.dq_peer, t.orecv, "x")
+
+    def kv_group(g):
+        while pre_sent:
+            slot = pre_sent.pop()
+            used[slot].wait_send()
+            used[slot] = None
+        col = pl.ds(g * 256, 256)
+        v = t_dot(t.norm_m[...], t.dkvp[:, col])
+        v += t_dot(t.norm_l[...], t.dkvl[:, col])
+        buffer["K"][..., col] = v.astype(BF).reshape(2, 2, 2, 2, 2, 32, 256)
+        if g == 1:
+            start("K")
+        if g == 3:
+            start("W")
+
+    def latent_back():
+        need(n.wk, n.wv)
+        arrive(n.dq_recv)
+        latent_back_body(
+            t.latent, t.norm_l, t.dkvl, t.oo, t.orecv, t.residual,
+            t.wq, t.wu.at[0], t.wu.at[1], src.lg, t.residual,
+            buffer["Q"].at[..., pl.ds(16, 16), :], vs.at[0, pl.ds(2, 2)],
+        )
+        send_late(pl.ds(16, 16), "Q")
+        t.ffn_in[...] = t.residual[...].astype(BF)
+        store(t.ffn_in, latents_grad)
+
+    def patch_back(i):
+        need(n.wk, n.wv)
+        at = pl.ds(i * size, size)
+        dkv = t.dkvp
+        grad = dot_t(dkv[at, :INNER], t.wu[0]) + dot_t(dkv[at, INNER:], t.wu[1])
+        unit, scale = centred(t.patch[at].astype(F32))
+        sums = t.sums
+        a, b = column_sum(grad * unit), column_sum(grad)
+        if i > 0:
+            a, b = a + sums[0:1, :], b + sums[1:2, :]
+        sums[0:1, :] = a
+        sums[1:2, :] = b
+        dkv[at] = norm_back(unit, scale, src.mg[...], grad).astype(BF)
+        store(dkv.at[at], patches_low.at[at])
+        if i == 3:
+            vs[0, 0:2, :] = sums[...]
+            vs[0, 6:8, :] = jnp.zeros((2, vs.shape[2]), F32)
+            arriving["V"] = send(vs.at[0], vr.at[0], vec_order[0])
+
+    simple = {"fi": first, "cb": combine, "fb": ffn_back, "ow": output_group, "lat": latent_back}
+    simple["+V"] = take_vector
+    for item in PLAN:
+        if item in simple:
+            simple[item]()
+        elif item[0] == "+":
+            take(item[1:])
+        elif item[:2] == "at":
+            a, b = item[2:].split(":")
+            attend_back(int(a), int(b))
+        elif item[:2] == "af":
+            a, b = item[2:].split(":")
+            attend(int(a), int(b))
+        elif item[:2] == "md":
+            media(int(item[2:]))
+        elif item[:2] == "kv":
+            kv_group(int(item[2:]))
+        elif item[:2] == "pt":
+            patch_back(int(item[2:]))
+        else:
+            {"j": ffn, "d": down_group, "u": up_group}[item[0]](int(item[1:]))
+    for copy in stores:
+        copy.wait()
+    for copy in used:
+        if copy is not None:
+            copy.wait_send()
+
+
+def last_body(
+    patches_in, fresh, latents_in, fin, vec,
+    patches_grad, new_latents, latents_grad, up, down, key, value, out, query, *thin,
+):
+    patches_grad[...] = patches_in[...].astype(F32)
+    new_latents[...] = fresh[...]
+    latents_grad[...] = latents_in[...].astype(F32)
+
+    @pl.when(pl.program_id(0) == 0)
+    def _():
+        for g in range(4):
+            up[:, g * 1024 : (g + 1) * 1024] = fin[4 + g]
+            for k in range(4):
+                down[k * 32 : (k + 1) * 32, g * 256 : (g + 1) * 256] = fin[
+                    g, :, k * 256 : (k + 1) * 256
+                ]
+        key[...] = fin[8, :, :INNER]
+        value[...] = fin[8, :, INNER:]
+        out[...] = fin[9, 0:16]
+        query[0:16] = fin[9, 16:32, :INNER]
+        query[16:32] = fin[9, 16:32, INNER:]
+        place = lax.axis_index("img") * 2 + lax.axis_index("lat")
+        width = vec.shape[1]
+        turned = pltpu.roll(vec[...], width - place * 32, 1)
+        for i, ref in enumerate(thin):
+            ref[...] = turned[i : i + 1, :32]
 
 
 def swap_lat(v):
@@ -609,12 +1191,107 @@
     )
 
 
+def fits(mesh):
+    return mesh.shape["img"] == 16 and mesh.shape["lat"] == 2
+
+
+def quick(
+    count,
+    patches,
+    latents,
+    cotangent,
+    doc_images,
+    doc_device,
+    query_weight,
+    key_weight,
+    value_weight,
+    output_weight,
+    up_weight,
+    down_weight,
+    media_gain,
+    media_bias,
+    latent_gain,
+    latent_bias,
+    ffn_gain,
+    ffn_bias,
+):
+    slots, own_patches, width = patches.shape
+    own_latents = latents.shape[1]
+    hidden = up_weight.shape[1]
+    np_, nl = slots * own_patches, slots * own_latents
+    patch = patches.reshape(np_, width)
+    latent = latents.reshape(nl, width)
+    cot = cotangent.reshape(nl, width)
+    mg, mb = media_gain.reshape(1, width), media_bias.reshape(1, width)
+    lg, lb = latent_gain.reshape(1, width), latent_bias.reshape(1, width)
+    fg, fb = ffn_gain.reshape(1, width), ffn_bias.reshape(1, width)
+    sspec = pl.BlockSpec(memory_space=pltpu.SMEM)
+    vmem = pl.BlockSpec(memory_space=pltpu.VMEM)
+    hbm = pl.BlockSpec(memory_space=pl.ANY)
+    names, scratch = main_scratch(nl, np_, width, hidden)
+    given = (
+        latent, query_weight, cot, patch, output_weight, key_weight, value_weight, up_weight,
+        down_weight, doc_images, doc_device, fg, fb, mg, mb, lg, lb,
+    )
+    fin, vec, patches_low, latents_low, new_latents = pl.pallas_call(
+        partial(main_body, names),
+        in_specs=[hbm] * 9 + [sspec] * 2 + [vmem] * 6,
+        out_specs=[vmem, vmem, hbm, hbm, hbm],
+        out_shape=[
+            struct((10,) + BLOCK, F32),
+            struct((8, width), F32),
+            struct((np_, width), BF),
+            struct((nl, width), BF),
+            struct((nl, width), BF),
+        ],
+        scratch_shapes=scratch,
+        compiler_params=pltpu.CompilerParams(
+            collective_id=0, has_side_effects=True, vmem_limit_bytes=60 * 1024 * 1024
+        ),
+    )(*given)
+    d = 2 * count
+    small = [
+        (width // d, hidden),
+        (hidden // d, width),
+        (width // d, INNER),
+        (width // d, INNER),
+        (INNER // d, width),
+        (width // d, INNER),
+    ] + [(1, width // d)] * 6
+    parts = 8
+    piece, long = rows(nl // parts, width), rows(np_ // parts, width)
+    patches_grad, fresh, latents_out, up_sum, down_sum, key_sum, value_sum, out_sum, query_sum, *thin = call(
+        last_body,
+        (parts,),
+        [long, piece, piece, whole((10,) + BLOCK), whole((8, width))],
+        [
+            (struct((np_, width), F32), long),
+            (struct((nl, width), BF), piece),
+            (struct((nl, width), F32), piece),
+        ]
+        + [(struct(shape, F32), whole(shape)) for shape in small],
+        (patches_low, new_latents, latents_low, fin, vec),
+        0,
+    )
+    return (
+        fresh.reshape(latents.shape),
+        patches_grad.reshape(patches.shape),
+        latents_out.reshape(latents.shape),
+        query_sum,
+        key_sum,
+        value_sum,
+        out_sum,
+        up_sum,
+        down_sum,
+    ) + tuple(v.reshape(-1) for v in thin)
+
+
 def solution(mesh):
     split = P("img", "lat", None)
     both = P(("img", "lat"), None)
     line = P(("img", "lat"))
     return jax.shard_map(
-        partial(local, mesh.shape["img"]),
+        partial(quick if fits(mesh) else local, mesh.shape["img"]),
         mesh=mesh,
         in_specs=(split,) * 3 + (P(),) * 14,
         out_specs=(split,) * 3 + (both,) * 6 + (line,) * 6,

time: 391 us -> 149 us (0.38)
  waiting for transfers between devices: 175 us -> 0 us
  starting transfers between devices: 70.6 us -> 0 us
  Pallas kernels: 88.8 us -> 148 us
  local copies, waits for them, and re-layouts: 35.5 us -> 0 us
  other arithmetic: 17.7 us -> 0 us
    ppermute x66 -> x0, waiting for transfers between devices: 175 us -> none  [the longest x60 167 us: halving_sum(): got = lax.ppermute(out, name, pairs)]
    pallas_call x0 -> x1, Pallas kernels: none -> 141 us  [quick(): pl.pallas_call(partial(main_body, names), in_specs=[hbm] * 9 + [sspec] *...]
    pallas_call x10 -> x1, Pallas kernels: 88.8 us -> 7.81 us  [call(): pl.pallas_call(body, grid=grid, in_specs=ins, out_specs=[o[1] for o in ou...]
    ppermute x66 -> x0, starting transfers between devices: 70.6 us -> none  [the longest x60 63.1 us: halving_sum(): got = lax.ppermute(out, name, pairs)]
    dynamic_slice x22 -> x0, local copies, waits for them, and re-layouts: 19.9 us -> none  [the longest x12 10.7 us: halving_sum(): out = lax.dynamic_index_in_dim(v, 1 - bit, dim, keepdims=False)]
    convert_element_type x44 -> x0, other arithmetic: 12 us -> none  [halving_sum(): v = v.astype(BF)]
    slice x9 -> x0, local copies, waits for them, and re-layouts: 9.46 us -> none  [reduce_parts(): v[:, a:b]]
  transfers between devices with their start and end apart: 66 -> 0, of which waited for: 36 -> 0; matrix products, arithmetic and copies ran while one was open for 11% -> 0% of each run, Pallas kernels for 10% -> 0%
where the time goes in v3:
time: 149 us
  Pallas kernels  148 us (99%)
    pallas_call x1, Pallas kernels, quick(): pl.pallas_call(partial(main_body, names), in_specs=[hbm] * 9 + [sspec] *...  141 us
    pallas_call x1, Pallas kernels, call(): pl.pallas_call(body, grid=grid, in_specs=ins, out_specs=[o[1] for o in ou...  7.81 us

profile of v3, /device:TPU:0, one launch (start us, length us, event | category | flops | bytes accessed | tf_op | source)
XLA Modules:
  0.0 149.2 jit_solution(1496861284182150673)
XLA Ops:
  0.7 140.5 %shard_map.280 = (f32[10,32,1024]{2,1,0:T(8,128)}, f32[8,1024]{1,0:T(8,128)}, bf16[1024,1024]{1,0:T(8,128)(2,1)}, bf16[256,1024]{1,0:T(8,128)(2,1)}, bf16[256,1024]{1,0:T(8,128)(2,1)}) custom-call(bf16[256,1024]{1,0:T(8,128)(2,1)} %bitcast.19, bf16[1024,512]{1,0:T(8,128)(2,1)} %refs_1_.1, bf16[256,1024]{1,0:T(8,128)(2,1)} %bitcast.20, ...), custom_call_target="tpu_custom_call" | custom-call | tf_op jit(solution)/shard_map/pallas_call | solution.py:1236
  141.2 7.8 %shard_map.281 = (f32[1024,1024]{1,0:T(8,128)}, bf16[256,1024]{1,0:T(8,128)(2,1)}, f32[256,1024]{1,0:T(8,128)}, f32[32,4096]{1,0:T(8,128)}, f32[128,1024]{1,0:T(...) custom-call(bf16[1024,1024]{1,0:T(8,128)(2,1)} %get-tuple-element.35, ...), custom_call_target="tpu_custom_call" | custom-call | bytes 11567872 | tf_op jit(solution)/shard_map/pallas_call | solution.py:37
